TPU v7x, 256 devices: a whole 4x4x8 slice. The times are simulated.
256 devices in a mesh: chan: 32 (over z, y_lo, core), win: 8 (over x, y_hi).
Axes of the slice: x: 4, y: 4 (y_hi: 2, y_lo: 2; y = y_hi * 2 + y_lo), z: 8, core: 2. Of those that a mesh axis runs over, the one named last changes fastest.
Arguments:
- spectra: bfloat16 [16, 2048, 2, 2048], P('win', 'chan'), may hold values from -180 to 180, as said below
- band_offsets: int32 [32, 2], P('chan'), may hold values from -256 to 256, as said below
- window_keep: int32 [16], P('win'), may hold values 0 or 1
- chan_dist: int32 [2048], replicated, may hold values from 0 to 2047, as said below
Outputs:
- linear_stack: float32 [2048, 2, 1024], P('chan')
- phase_stack: float32 [2048, 2, 1024], P('chan')
- distance_gather: float32 [1024, 1024], P('chan')
Inputs may be any that keep to these rules, and one draw needn't show every extreme that they name: `spectra`: spectra with row and frequency scales. `band_offsets`: each block's 2 offsets are nonzero; the first and the last block each hold both +256 and -256. `chan_dist`: never falls from one channel to the next, by steps of 0, 1 or 2; the first channel has 0 and the last has 2047.
All inputs are finite; a program needn't handle non-finite values. No bound on the sum of `window_keep` on one device may be relied on, other than what follows from the above.
Results may differ from a plain program's by a relative error of at most 0.015.
Values may be sent and summed in bfloat16 or wider, within the bound.
A program may use at most 64 MiB of HBM per device.

v0:
```python
import math

import jax
import jax.numpy as jnp
from jax import lax
from jax.sharding import PartitionSpec as P

LAGS = 1024
HALF = 256
NBIN = 32


EPS = 1e-06
FLOOR = 0.1


def from_behind(value, axis, steps):
    count = lax.axis_size(axis)
    pairs = [(source, (source + steps) % count) for source in range(count)]
    return lax.ppermute(value, axis, pairs)


def dft_table(freqs, first_lag, count):
    bins = jnp.arange(freqs, dtype=jnp.int32)[:, None]
    shifts = first_lag + jnp.arange(count, dtype=jnp.int32)[None, :]
    turns = jnp.mod(bins * shifts, 2 * freqs).astype(jnp.float32)
    angle = turns * (math.pi / freqs)
    cosine = jnp.cos(angle) / math.sqrt(freqs)
    sine = jnp.sin(angle) / math.sqrt(freqs)
    upper = jnp.concatenate([cosine, sine], axis=1)
    lower = jnp.concatenate([-sine, cosine], axis=1)
    return jnp.concatenate([upper, lower], axis=0).astype(jnp.bfloat16)


def whiten(spectra):
    values = spectra.astype(jnp.float32)
    power = jnp.mean(values[:, :, 0] ** 2 + values[:, :, 1] ** 2, axis=-1)
    return (values * lax.rsqrt(power + EPS)[:, :, None, None]).astype(jnp.bfloat16)


def cross_pair(mine, other):
    mine = mine.astype(jnp.float32)
    other = other.astype(jnp.float32)
    real = mine[..., 0, :] * other[..., 0, :] + mine[..., 1, :] * other[..., 1, :]
    imag = mine[..., 1, :] * other[..., 0, :] - mine[..., 0, :] * other[..., 1, :]
    return jnp.concatenate([real, imag], axis=-1).astype(jnp.bfloat16)


def finish(lin_sum, re_sum, im_sum, member, windows):
    linear = lin_sum / math.sqrt(windows)
    phased = linear * jnp.sqrt(re_sum * re_sum + im_sum * im_sum) / windows
    binned = jnp.dot(
        member, linear, precision=lax.Precision.HIGHEST, preferred_element_type=jnp.float32
    )
    return (linear, phased, binned)


def local(spectra, band_offsets, window_keep, chan_dist):
    win_dev, ch_dev, _, freqs = spectra.shape
    n_off = band_offsets.shape[1]
    windows = win_dev * lax.axis_size("win")
    channels = ch_dev * lax.axis_size("chan")
    lags = LAGS
    white = whiten(spectra)
    reach = (HALF + ch_dev - 1) // ch_dev
    lower_parts = []
    upper_parts = []
    for step in range(1, reach + 1):
        lower_parts.append(from_behind(white, "chan", step))
        upper_parts.append(from_behind(white, "chan", -step))
    joined = jnp.concatenate(lower_parts[::-1] + [white] + upper_parts, axis=1)
    pieces = []
    for which in range(n_off):
        start = HALF + band_offsets[0, which]
        other = lax.dynamic_slice_in_dim(joined, start, ch_dev, 1)
        pieces.append(cross_pair(white, other))
    cross = jnp.stack(pieces, axis=2).reshape(win_dev * ch_dev * n_off, 2 * freqs)
    weight = window_keep.astype(jnp.float32)[:, None, None]
    width = math.gcd(lags, 128)
    lin_parts = []
    re_parts = []
    im_parts = []
    for first in range(0, lags, width):
        table = dft_table(freqs, first - lags // 2, width)
        analytic = jnp.dot(cross, table, preferred_element_type=jnp.float32)
        analytic = analytic.reshape(win_dev, ch_dev * n_off, 2 * width)
        real = analytic[..., :width]
        imag = analytic[..., width:]
        scale = weight / jnp.maximum(jnp.sqrt(real * real + imag * imag), FLOOR)
        lin_parts.append(jnp.sum(weight * real, axis=0))
        re_parts.append(jnp.sum(scale * real, axis=0))
        im_parts.append(jnp.sum(scale * imag, axis=0))
    lin_sum = jnp.concatenate(lin_parts, axis=1)
    re_sum = jnp.concatenate(re_parts, axis=1)
    im_sum = jnp.concatenate(im_parts, axis=1)
    own = lax.axis_index("chan") * ch_dev + jnp.arange(ch_dev, dtype=jnp.int32)
    partner = jnp.mod(own[:, None] + band_offsets[0][None, :], channels)
    every = jnp.arange(channels, dtype=jnp.int32)
    own_dist = jnp.sum(jnp.where(own[:, None] == every[None, :], chan_dist[None, :], 0), axis=1)
    partner_dist = jnp.sum(
        jnp.where(partner[:, :, None] == every[None, None, :], chan_dist[None, None, :], 0), axis=2
    )
    bins = jnp.minimum(jnp.abs(partner_dist - own_dist[:, None]), NBIN - 1).reshape(-1)
    member = (jnp.arange(NBIN, dtype=jnp.int32)[:, None] == bins[None, :]).astype(jnp.float32)
    lin_sum, re_sum, im_sum = lax.psum((lin_sum, re_sum, im_sum), "win")
    linear, phased, binned = finish(lin_sum, re_sum, im_sum, member, windows)
    return (linear.reshape(ch_dev, n_off, lags), phased.reshape(ch_dev, n_off, lags), binned)


def solution(mesh):
    in_specs = (P("win", "chan", None, None), P("chan", None), P("win"), P())
    out_specs = (P("chan", None, None), P("chan", None, None), P("chan", None))
    return jax.shard_map(local, mesh=mesh, in_specs=in_specs, out_specs=out_specs, check_vma=False)
```

profile of v0, /device:TPU:32, one launch (start us, length us, event | category | flops | bytes accessed | tf_op | source)
XLA Modules:
  0.0 289.2 jit_solution(5353202751727358195)
XLA Ops:
  7.2 2.5 convert_element_type.117
  9.7 2.9 %fusion.105 = f32[2,64]{1,0:T(2,128)S(1)} fusion(f32[2,64,2,2048]{3,2,1,0:T(2,128)S(1)} %convert_element_type.117), kind=kLoop, calls=%fused_computation.173 | loop fusion | flops 1048448 | bytes 2097664 | tf_op jit(solution)/shard_map/reduce_sum | solution.py:37
  12.7 2.2 fusion.125
  14.8 1.9 collective-permute-start
  16.7 0.7 collective-permute-start.1
  17.5 1.8 collective-permute-start.2
  19.3 0.8 collective-permute-start.3
  20.1 2.3 collective-permute-start.4
  22.4 5.2 %fusion.106 = (bf16[2048,128]{1,0:T(8,128)(2,1)}, bf16[2048,128]{1,0:T(8,128)(2,1)}, bf16[2048,128]{1,0:T(8,128)(2,1)}) fusion(s32[128]{0:T(128)S(1)} %iota_add_fusion.7), kind=kLoop, calls=%fused_computation.174 | loop fusion | flops 5242880 | bytes 1573376 | tf_op jit(solution)/shard_map/convert.47
  27.6 5.2 %fusion.108 = (bf16[2048,128]{1,0:T(8,128)(2,1)}, bf16[2048,128]{1,0:T(8,128)(2,1)}, bf16[2048,128]{1,0:T(8,128)(2,1)}) fusion(s32[128]{0:T(128)S(1)} %iota_add_fusion.5), kind=kLoop, calls=%fused_computation.176 | loop fusion | flops 5242880 | bytes 1573376 | tf_op jit(solution)/shard_map/convert.35
  32.9 5.2 %fusion.109 = (bf16[2048,128]{1,0:T(8,128)(2,1)}, bf16[2048,128]{1,0:T(8,128)(2,1)}, bf16[2048,128]{1,0:T(8,128)(2,1)}) fusion(s32[128]{0:T(128)S(1)} %iota_add_fusion.4), kind=kLoop, calls=%fused_computation.177 | loop fusion | flops 5242880 | bytes 1573376 | tf_op jit(solution)/shard_map/convert.29
  38.1 5.2 %fusion.112 = (bf16[2048,128]{1,0:T(8,128)(2,1)}, bf16[2048,128]{1,0:T(8,128)(2,1)}, bf16[2048,128]{1,0:T(8,128)(2,1)}) fusion(s32[128]{0:T(128)S(1)} %iota_add_fusion.2), kind=kLoop, calls=%fused_computation.180 | loop fusion | flops 5242880 | bytes 1573376 | tf_op jit(solution)/shard_map/convert.11
  43.3 5.2 %fusion.113 = (bf16[2048,128]{1,0:T(8,128)(2,1)}, bf16[2048,128]{1,0:T(8,128)(2,1)}, bf16[2048,128]{1,0:T(8,128)(2,1)}) fusion(s32[128]{0:T(128)S(1)} %iota_add_fusion.1), kind=kLoop, calls=%fused_computation.181 | loop fusion | flops 5242880 | bytes 1573376 | tf_op jit(solution)/shard_map/convert.5
  48.5 5.2 %fusion.107 = (bf16[2048,128]{1,0:T(8,128)(2,1)}, bf16[2048,128]{1,0:T(8,128)(2,1)}, bf16[2048,128]{1,0:T(8,128)(2,1)}) fusion(s32[128]{0:T(128)S(1)} %iota_add_fusion.6), kind=kLoop, calls=%fused_computation.175 | loop fusion | flops 5242880 | bytes 1573376 | tf_op jit(solution)/shard_map/convert.41
  53.7 5.2 %fusion.111 = (bf16[2048,128]{1,0:T(8,128)(2,1)}, bf16[2048,128]{1,0:T(8,128)(2,1)}, bf16[2048,128]{1,0:T(8,128)(2,1)}) fusion(s32[128]{0:T(128)S(1)} %iota_add_fusion.3), kind=kLoop, calls=%fused_computation.179 | loop fusion | flops 5242880 | bytes 1573376 | tf_op jit(solution)/shard_map/convert.17
  58.9 4.6 %fusion.110 = bf16[2048,128]{1,0:T(8,128)(2,1)} fusion(), kind=kLoop, calls=%fused_computation.178 | loop fusion | flops 4194304 | bytes 524288 | tf_op jit(solution)/shard_map/convert.23
  63.6 0.6 fusion.126
  66.8 5.4 %negate_convert_fusion.3 = (bf16[2048,128]{1,0:T(8,128)(2,1)}, bf16[2048,128]{1,0:T(8,128)(2,1)}) fusion(), kind=kLoop, calls=%fused_computation.134 | loop fusion | flops 4980736 | bytes 1048576 | tf_op jit(solution)/shard_map/convert.20
  72.2 0.2 collective-permute-start.5
  72.4 1.9 constant_dynamic-update-slice_fusion.8
  74.3 1.1 collective-permute-start.6
  75.4 2.0 constant_dynamic-update-slice_fusion.7
  77.5 9.8 %collective-permute-done.2 = bf16[2,64,2,2048]{3,2,1,0:T(2,128)(2,1)} collective-permute-done((bf16[2,64,2,2048]{3,2,1,0:T(2,128)(2,1)}, bf16[2,64,2,2048]{3,2,1,0:T(2,128)(2,1)}, u32[]{:S(2)}, u32[]{:S(2)}) %collective-permute-start.2) | collective-permute-done | bytes 1048608 | tf_op jit(solution)/shard_map/ppermute | solution.py:20
  87.2 3.9 %collective-permute-start.7 = (bf16[2,64,2,2048]{3,2,1,0:T(2,128)(2,1)}, bf16[2,64,2,2048]{3,2,1,0:T(2,128)(2,1)S(1)}, u32[]{:S(2)}, u32[]{:S(2)}) collective-permute-start(bf16[2,64,2,2048]{3,2,1,0:T(2,128)(2,1)} %get-tuple-element.46), channel_id=1, source_target_pairs={{0,224},{8,232},{16,240},{24,248},{32,0},{40,8},{48,16},{56,24},{6... | collective-permute-start | bytes 3145736 | tf_op jit(solution)/shard_map/ppermute | solution.py:20
  91.1 2.0 constant_dynamic-update-slice_fusion.6
  93.2 4.2 %collective-permute-done.3 = bf16[2,64,2,2048]{3,2,1,0:T(2,128)(2,1)} collective-permute-done((bf16[2,64,2,2048]{3,2,1,0:T(2,128)(2,1)}, bf16[2,64,2,2048]{3,2,1,0:T(2,128)(2,1)}, u32[]{:S(2)}, u32[]{:S(2)}) %collective-permute-start.3) | collective-permute-done | bytes 1048608 | tf_op jit(solution)/shard_map/ppermute | solution.py:20
  97.3 2.0 constant_dynamic-update-slice_fusion.5
  99.4 2.0 constant_dynamic-update-slice_fusion.4
  101.4 0.8 constant_dynamic-update-slice_fusion.3
  102.2 17.5 %collective-permute-done.5 = bf16[2,64,2,2048]{3,2,1,0:T(2,128)(2,1)S(1)} collective-permute-done((bf16[2,64,2,2048]{3,2,1,0:T(2,128)(2,1)}, bf16[2,64,2,2048]{3,2,1,0:T(2,128)(2,1)S(1)}, u32[]{:S(2)}, u32[]{:S(2)}) %collective-permute-start.5) | collective-permute-done | bytes 1048608 | tf_op jit(solution)/shard_map/ppermute | solution.py:20
  119.6 0.8 constant_dynamic-update-slice_fusion.2
  120.5 10.4 %collective-permute-done.6 = bf16[2,64,2,2048]{3,2,1,0:T(2,128)(2,1)S(1)} collective-permute-done((bf16[2,64,2,2048]{3,2,1,0:T(2,128)(2,1)}, bf16[2,64,2,2048]{3,2,1,0:T(2,128)(2,1)S(1)}, u32[]{:S(2)}, u32[]{:S(2)}) %collective-permute-start.6) | collective-permute-done | bytes 1048608 | tf_op jit(solution)/shard_map/ppermute | solution.py:20
  130.8 0.8 constant_dynamic-update-slice_fusion.1
  131.6 12.3 %collective-permute-done.7 = bf16[2,64,2,2048]{3,2,1,0:T(2,128)(2,1)S(1)} collective-permute-done((bf16[2,64,2,2048]{3,2,1,0:T(2,128)(2,1)}, bf16[2,64,2,2048]{3,2,1,0:T(2,128)(2,1)S(1)}, u32[]{:S(2)}, u32[]{:S(2)}) %collective-permute-start.7) | collective-permute-done | bytes 1048608 | tf_op jit(solution)/shard_map/ppermute | solution.py:20
  143.9 0.8 constant_dynamic-update-slice_fusion
  144.7 2.4 dynamic-slice_convert_fusion.1
  147.1 6.2 %add_convert_fusion.1 = (bf16[2,64,1,2048]{3,2,1,0:T(2,128)(2,1)S(1)}, bf16[2,64,1,2048]{3,2,1,0:T(2,128)(2,1)S(1)}, bf16[2,64,1,2048]{3,2,1,0:T(2,128)(2,1)S(1)}, bf16[2,64,1,2048]{3,2,1,0:T(2,128)(2,1)S(1)}) fusion(f32[2,64,2,2048]{3,2,1,0:T(2,128)S(1)} %get-tuple-element.47, f32[2,64,2,2048]{3,2,1,0:T(2,128)S(1)} %get-tuple-element.45, ...), kind=kLoop, calls=%fused_computation.163 | loop fusion | flops 4194304 | bytes 8388608 | tf_op jit(solution)/shard_map/convert.50
  153.3 4.8 %maximum_maximum_fusion = bf16[2,64,2,4096]{3,2,1,0:T(2,128)(2,1)S(1)} fusion(bf16[2,64,1,2048]{3,2,1,0:T(2,128)(2,1)S(1)} %get-tuple-element.53, bf16[2,64,1,2048]{3,2,1,0:T(2,128)(2,1)S(1)} %get-tuple-element.54, bf16[2,64,1,2048]{3,2,1,0:T(2,128)(2,1)S(1)} %get-tuple-element.50, bf16[2,64,1,2048]{3,2,1,0:T(2,128)(2,1)S(1)} %get-tuple-element.49), kind=kLoop, calls=%fused_computation | loop fusion | flops 8388608 | bytes 4194304 | tf_op jit(solution)/shard_map/stack | solution.py:77
  158.2 2.2 dot_general.29
  160.4 2.7 fusion
  163.4 0.7 fusion.14
  164.1 0.3 copy-done.14
  164.6 0.2 copy-done.16
  164.7 0.7 fusion.21
  165.4 0.3 copy-done.17
  166.1 0.7 fusion.42
  166.8 0.3 copy-done.20
  167.4 0.7 fusion.49
  168.1 0.3 copy-done.23
  168.8 0.7 fusion.7
  169.5 0.3 copy-done.26
  170.1 0.7 fusion.28
  170.9 0.3 copy-done.6
  171.5 0.7 fusion.35
  172.2 0.7 multiply_reduce_fusion.10
  173.3 0.6 copy-done.5
  174.1 0.2 copy-done.3
  174.3 0.2 select_reduce_fusion.1
  174.6 0.3 select_reduce_fusion
  175.1 102.2 %all-reduce.3.cloned.1.call-done = (f32[128,1024]{1,0:T(8,128)}, f32[128,1024]{1,0:T(8,128)}, f32[128,1024]{1,0:T(8,128)}) async-done(((f32[128,1024]{1,0:T(8,128)}, f32[128,1024]{1,0:T(8,128)}, f32[128,1024]{1,0:T(8,128)}), (f32[128,1024]{1,0:T(8,128)}, f32[128,1024]{1,0:T(8,128)}, f32[128,1024]{1,0:T(8,128)})) %all-reduce.3.cloned.1.call-update) | async-done | bytes 1572880 | tf_op jit(solution)/shard_map/psum | solution.py:105
  277.3 1.6 multiply_multiply_fusion
  279.0 1.1 reshape.198
  280.1 1.1 reshape.199
  281.2 1.0 fusion.114
  (98 shorter events, 2.8 us)
Async XLA Ops:
  7.2 5.5 %copy-start = (bf16[2,64,2,2048]{3,2,1,0:T(2,128)(2,1)S(1)}, bf16[2,64,2,2048]{3,2,1,0:T(2,128)(2,1)}, u32[]{:S(2)}) copy-start(bf16[2,64,2,2048]{3,2,1,0:T(2,128)(2,1)} %param.4) | copy-start | bytes 3145732
  7.2 270.1 %all-reduce.3.cloned.1.call-start = ((), (), s32[]{:S(2)}) async-start(), calls=%async_computation | async-start | bytes 3145728 | tf_op jit(solution)/shard_map/psum | solution.py:105
  14.8 57.3 %collective-permute-start = (bf16[2,64,2,2048]{3,2,1,0:T(2,128)(2,1)}, bf16[2,64,2,2048]{3,2,1,0:T(2,128)(2,1)}, u32[]{:S(2)}, u32[]{:S(2)}) collective-permute-start(bf16[2,64,2,2048]{3,2,1,0:T(2,128)(2,1)} %get-tuple-element.46), channel_id=1, source_target_pairs={{0,32},{8,40},{16,48},{24,56},{32,64},{40,72},{48,80},{56,88},{64,... | collective-permute-start | bytes 3145736 | tf_op jit(solution)/shard_map/ppermute | solution.py:20
  16.7 57.6 %collective-permute-start.1 = (bf16[2,64,2,2048]{3,2,1,0:T(2,128)(2,1)}, bf16[2,64,2,2048]{3,2,1,0:T(2,128)(2,1)}, u32[]{:S(2)}, u32[]{:S(2)}) collective-permute-start(bf16[2,64,2,2048]{3,2,1,0:T(2,128)(2,1)} %get-tuple-element.46), channel_id=1, source_target_pairs={{0,24},{8,32},{16,40},{24,48},{32,56},{40,64},{48,72},{56,80},{64,... | collective-permute-start | bytes 3145736 | tf_op jit(solution)/shard_map/ppermute | solution.py:20
  17.5 69.8 %collective-permute-start.2 = (bf16[2,64,2,2048]{3,2,1,0:T(2,128)(2,1)}, bf16[2,64,2,2048]{3,2,1,0:T(2,128)(2,1)}, u32[]{:S(2)}, u32[]{:S(2)}) collective-permute-start(bf16[2,64,2,2048]{3,2,1,0:T(2,128)(2,1)} %get-tuple-element.46), channel_id=1, source_target_pairs={{0,16},{8,24},{16,32},{24,40},{32,48},{40,56},{48,64},{56,72},{64,... | collective-permute-start | bytes 3145736 | tf_op jit(solution)/shard_map/ppermute | solution.py:20
  19.3 78.0 %collective-permute-start.3 = (bf16[2,64,2,2048]{3,2,1,0:T(2,128)(2,1)}, bf16[2,64,2,2048]{3,2,1,0:T(2,128)(2,1)}, u32[]{:S(2)}, u32[]{:S(2)}) collective-permute-start(bf16[2,64,2,2048]{3,2,1,0:T(2,128)(2,1)} %get-tuple-element.46), channel_id=1, source_target_pairs={{0,8},{8,16},{16,24},{24,32},{32,40},{40,48},{48,56},{56,64},{64,7... | collective-permute-start | bytes 3145736 | tf_op jit(solution)/shard_map/ppermute | solution.py:20
  20.1 81.3 %collective-permute-start.4 = (bf16[2,64,2,2048]{3,2,1,0:T(2,128)(2,1)}, bf16[2,64,2,2048]{3,2,1,0:T(2,128)(2,1)S(1)}, u32[]{:S(2)}, u32[]{:S(2)}) collective-permute-start(bf16[2,64,2,2048]{3,2,1,0:T(2,128)(2,1)} %get-tuple-element.46), channel_id=1, source_target_pairs={{0,248},{8,0},{16,8},{24,16},{32,24},{40,32},{48,40},{56,48},{64,5... | collective-permute-start | bytes 3145736 | tf_op jit(solution)/shard_map/ppermute | solution.py:20
  48.5 15.1 %copy-start.30 = (s32[1,2]{1,0:T(1,128)S(1)}, s32[1,2]{1,0:T(1,128)}, u32[]{:S(2)}) copy-start(s32[1,2]{1,0:T(1,128)} %param.5) | copy-start | bytes 28
  48.5 18.3 %copy-start.31 = (s32[2]{0:T(128)S(1)}, s32[2]{0:T(128)}, u32[]{:S(2)}) copy-start(s32[2]{0:T(128)} %param.6) | copy-start | bytes 28
  72.2 47.5 %collective-permute-start.5 = (bf16[2,64,2,2048]{3,2,1,0:T(2,128)(2,1)}, bf16[2,64,2,2048]{3,2,1,0:T(2,128)(2,1)S(1)}, u32[]{:S(2)}, u32[]{:S(2)}) collective-permute-start(bf16[2,64,2,2048]{3,2,1,0:T(2,128)(2,1)} %get-tuple-element.46), channel_id=1, source_target_pairs={{0,240},{8,248},{16,0},{24,8},{32,16},{40,24},{48,32},{56,40},{64,... | collective-permute-start | bytes 3145736 | tf_op jit(solution)/shard_map/ppermute | solution.py:20
  74.3 56.5 %collective-permute-start.6 = (bf16[2,64,2,2048]{3,2,1,0:T(2,128)(2,1)}, bf16[2,64,2,2048]{3,2,1,0:T(2,128)(2,1)S(1)}, u32[]{:S(2)}, u32[]{:S(2)}) collective-permute-start(bf16[2,64,2,2048]{3,2,1,0:T(2,128)(2,1)} %get-tuple-element.46), channel_id=1, source_target_pairs={{0,232},{8,240},{16,248},{24,0},{32,8},{40,16},{48,24},{56,32},{64... | collective-permute-start | bytes 3145736 | tf_op jit(solution)/shard_map/ppermute | solution.py:20
  87.2 56.7 %collective-permute-start.7 = (bf16[2,64,2,2048]{3,2,1,0:T(2,128)(2,1)}, bf16[2,64,2,2048]{3,2,1,0:T(2,128)(2,1)S(1)}, u32[]{:S(2)}, u32[]{:S(2)}) collective-permute-start(bf16[2,64,2,2048]{3,2,1,0:T(2,128)(2,1)} %get-tuple-element.46), channel_id=1, source_target_pairs={{0,224},{8,232},{16,240},{24,248},{32,0},{40,8},{48,16},{56,24},{6... | collective-permute-start | bytes 3145736 | tf_op jit(solution)/shard_map/ppermute | solution.py:20
  158.1 2.3 copy-start.9
  158.2 2.3 copy-start.10
  160.4 2.7 copy-start.2
  160.4 2.7 copy-start.11
  160.4 2.8 copy-start.12
  160.4 2.9 %copy-start.13 = (bf16[2048,128]{1,0:T(8,128)(2,1)S(1)}, bf16[2048,128]{1,0:T(8,128)(2,1)}, u32[]{:S(2)}) copy-start(bf16[2048,128]{1,0:T(8,128)(2,1)} %get-tuple-element.83) | copy-start | bytes 1572868
  163.4 1.0 copy-start.14
  163.4 1.2 copy-start.15
  163.4 1.4 copy-start.16
  164.7 1.0 copy-start.17
  164.7 1.2 copy-start.18
  164.7 1.4 copy-start.19
  166.1 1.0 copy-start.20
  166.1 1.2 copy-start.21
  166.1 1.4 copy-start.22
  167.4 1.0 copy-start.23
  167.4 1.2 copy-start.24
  167.4 1.4 copy-start.25
  168.8 1.0 copy-start.26
  168.8 1.2 copy-start.27
  168.8 1.4 copy-start.28
  170.1 1.0 copy-start.6
  170.1 1.2 copy-start.7
  170.1 1.4 copy-start.8
  173.0 1.3 copy-start.29
  173.1 0.8 copy-start.5
  173.2 0.8 copy-start.4
  173.3 0.9 copy-start.3
  277.3 3.8 %copy-start.1 = (f32[128,1024]{1,0:T(8,128)S(1)}, f32[128,1024]{1,0:T(8,128)}, u32[]{:S(2)}) copy-start(f32[128,1024]{1,0:T(8,128)} %get-tuple-element.42) | copy-start | bytes 1572868
Sparse Core Ops, SparseCore 0:
  174.4 102.8 all-reduce.2
where the time goes:
time: 295 us; the launch traced here: 289 us
  waiting for transfers between devices  156 us (53%)
  other arithmetic  70.5 us (24%)
  local copies, waits for them, and re-layouts  23.7 us (8%)
  between operations  17.4 us (6%)
  starting transfers between devices  12.8 us (4%)
  matrix products  8.58 us (3%)
    psum x1, waiting for transfers between devices, local(): lin_sum, re_sum, im_sum = lax.psum((lin_sum, re_sum, im_sum), 'win')  102 us
    ppermute x8, waiting for transfers between devices, from_behind(): return lax.ppermute(value, axis, pairs)  54 us
    another operation x10, other arithmetic  52.7 us
    unnamed x93, local copies, waits for them, and re-layouts  17.6 us
    ppermute x8, starting transfers between devices, from_behind(): return lax.ppermute(value, axis, pairs)  12.8 us
    dot_general x8, matrix products, local(): analytic = jnp.dot(cross, table, preferred_element_type=jnp.float32)  7.62 us
  transfers between devices with their start and end apart: 9, of which 6 were waited for; matrix products, arithmetic and copies ran while one was open for 21% of the time, Pallas kernels for 0%

commit v1 on v0

v1 whole, which is shorter than its diff:
```python
import functools
import math

import jax
import jax.numpy as jnp
from jax import lax
from jax.experimental import pallas as pl
from jax.experimental.pallas import tpu as pltpu
from jax.sharding import PartitionSpec as P

LAGS = 1024
NBIN = 32
EPS = 1e-06
FLOOR = 0.1

F = 2048
CH = 64
Q = 4
L = F // 128 // Q
KQ = L * 128
FINE = 32
MESH = pl.DeviceIdType.MESH


def whiten(spectra):
    values = spectra.astype(jnp.float32)
    power = jnp.mean(values[:, :, 0] ** 2 + values[:, :, 1] ** 2, axis=-1)
    return (values * lax.rsqrt(power + EPS)[:, :, None, None]).astype(jnp.bfloat16)


def turn(product):
    return jnp.bitwise_and(product, 2 * F - 1).astype(jnp.float32) * (math.pi / F)


def kernel(
    wt, offs, keep, member,
    lin_out, ph_out, bin_out,
    j0, j1, j2, j3, j32, ea, eb, table, x, acc, s,
    ra, rb, pa, pb, ra2, rb2, g,
    local_sem, send_sem, recv_sem,
):
    joined = (j0, j1, j2, j3)
    chan = lax.axis_index("chan")
    win = lax.axis_index("win")
    core = lax.rem(chan, 2)
    ylo = lax.rem(chan // 2, 2)
    xx = win // 2
    yhi = lax.rem(win, 2)
    yy = yhi * 2 + ylo
    base = chan - ylo * 2
    above = lax.rem(chan + 4, 32)
    below = lax.rem(chan + 28, 32)
    mate = chan + 1 - 2 * core
    across = chan + 2 - 4 * ylo
    own = ylo * 2 + core
    far = (1 - ylo) * 2 + core

    x_peer = [lax.rem(xx + d, 4) for d in (1, 2, 3)]
    y_peer = [lax.rem(yy + d, 4) for d in (1, 2, 3)]
    x_dev = [{"chan": chan, "win": p * 2 + yhi} for p in x_peer]
    y_dev = [{"chan": base + lax.rem(p, 2) * 2, "win": xx * 2 + p // 2} for p in y_peer]
    g_dev = [{"chan": chan, "win": win + 1 - 2 * yhi}] + [
        dev for p in x_peer for dev in (
            {"chan": chan, "win": p * 2 + yhi}, {"chan": chan, "win": p * 2 + 1 - yhi})
    ]

    barrier = pltpu.get_barrier_semaphore()
    greet = [{"chan": c, "win": win} for c in (above, below, mate)] + y_dev + x_dev + [
        {"chan": chan, "win": p * 2 + 1 - yhi} for p in x_peer
    ]
    for dev in greet:
        pl.semaphore_signal(barrier, inc=1, device_id=dev, device_id_type=MESH)
    pl.semaphore_wait(barrier, len(greet))

    count = [0]
    sent = []

    def send(src, dst, device):
        i = count[0]
        count[0] += 1
        copy = pltpu.make_async_remote_copy(
            src_ref=src, dst_ref=dst, send_sem=send_sem.at[i], recv_sem=recv_sem.at[i],
            device_id=device, device_id_type=MESH,
        )
        copy.start()
        sent.append(copy)
        return copy

    def near(c):
        return {"chan": c, "win": win}

    lanes = [pl.ds(q * L, L) for q in range(Q)]
    stay, cross_y, up, down, mate_own = [], [], [], [], []
    for q in range(Q):
        mine = wt.at[ylo, lanes[q]]
        copy = pltpu.make_async_copy(mine, joined[q].at[4 + own], local_sem.at[q])
        copy.start()
        stay.append(copy)
        cross_y.append(send(wt.at[1 - ylo, lanes[q]], joined[q].at[4 + own], near(across)))
        up.append(send(mine, joined[q].at[own], near(above)))
        down.append(send(mine, joined[q].at[8 + own], near(below)))
        mate_own.append(send(mine, joined[q].at[4 + own], near(mate)))

    lag = lax.broadcasted_iota(jnp.int32, (FINE, LAGS), 1) - LAGS // 2
    row = lax.broadcasted_iota(jnp.int32, (FINE, LAGS), 0)
    fine = turn(row * lag)
    eb[0] = jnp.cos(fine) * (1.0 / math.sqrt(F))
    eb[1] = jnp.sin(fine) * (1.0 / math.sqrt(F))
    for half in range(F // FINE // FINE):
        coarse = turn((row + half * FINE) * FINE * lag)
        ea[0, half * FINE:(half + 1) * FINE] = jnp.cos(coarse)
        ea[1, half * FINE:(half + 1) * FINE] = jnp.sin(coarse)

    per = KQ // FINE

    def fill(a, _):
        ca = ea[0, pl.ds(a, 1), :]
        sa = ea[1, pl.ds(a, 1), :]
        q2 = (a // per) * 2
        at = pl.ds(pl.multiple_of(lax.rem(a, per) * FINE, FINE), FINE)
        table[q2, at, :] = (eb[0] * ca - eb[1] * sa).astype(jnp.bfloat16)
        table[q2 + 1, at, :] = (eb[1] * ca + eb[0] * sa).astype(jnp.bfloat16)
        return 0

    lax.fori_loop(0, F // FINE, fill, 0)

    up_far, down_far, mate_far = [], [], []
    for q in range(Q):
        cross_y[q].wait_recv()
        mine = joined[q].at[4 + far]
        up_far.append(send(mine, joined[q].at[far], near(above)))
        down_far.append(send(mine, joined[q].at[8 + far], near(below)))
        mate_far.append(send(mine, joined[q].at[4 + far], near(mate)))

    def forward(q):
        for copy in (up[q], down[q], up_far[q], down_far[q]):
            copy.wait_recv()
        return [
            send(joined[q].at[pos], joined[q].at[pos], near(mate))
            for pos in (2 + core, 8 + core, 10 - 9 * core)
        ]

    starts = []
    for b in range(2):
        block = core + 2 * b
        which = jnp.where(block == own, 0, 1)
        for k in range(2):
            starts.append(((4 + block) * CH, (4 + block) * CH + jnp.where(
                block == own, offs[0, k], offs[1, k])))

    for q in range(Q):
        moved = forward(q)
        stay[q].wait()
        mate_own[q].wait_recv()
        mate_far[q].wait_recv()
        for copy in moved:
            copy.wait_recv()

        def widen(i, _):
            p = core + i
            at = pl.ds(pl.multiple_of(p * CH, CH), CH)
            for lg in range(L):
                for ri in range(2):
                    j32[lg * 2 + ri, at, :] = joined[q][p, lg, ri].astype(jnp.float32)
            return 0

        lax.fori_loop(0, 11, widen, 0)
        for r, (mine_at, other_at) in enumerate(starts):
            at_m = pl.ds(pl.multiple_of(mine_at, CH), CH)
            at_o = pl.ds(other_at, CH)
            for lg in range(L):
                mr, mi = j32[lg * 2, at_m, :], j32[lg * 2 + 1, at_m, :]
                orr, oi = j32[lg * 2, at_o, :], j32[lg * 2 + 1, at_o, :]
                real = (mr * orr + mi * oi).astype(jnp.bfloat16)
                imag = (mi * orr - mr * oi).astype(jnp.bfloat16)
                top = slice(r * CH, (r + 1) * CH)
                low = slice((4 + r) * CH, (5 + r) * CH)
                one = slice(lg * 128, (lg + 1) * 128)
                two = slice(KQ + lg * 128, KQ + (lg + 1) * 128)
                x[top, one] = real
                x[top, two] = -imag
                x[low, one] = imag
                x[low, two] = real

        def multiply(n, _):
            at = pl.ds(pl.multiple_of(n * 256, 256), 256)
            value = jnp.dot(x[:, :KQ], table[2 * q, :, at], preferred_element_type=jnp.float32)
            value += jnp.dot(x[:, KQ:], table[2 * q + 1, :, at], preferred_element_type=jnp.float32)
            if q == 0:
                acc[:, at] = value
            else:
                acc[:, at] += value
            return 0

        lax.fori_loop(0, LAGS // 256, multiply, 0)

    weight = jnp.where(ylo == 0, keep[0], keep[1]).astype(jnp.float32)
    for b in range(2):
        for k in range(2):
            def stack(i, _):
                r = (b * 2 + k) * CH + i * 16
                real = acc[pl.ds(pl.multiple_of(r, 16), 16), :]
                imag = acc[pl.ds(pl.multiple_of(4 * CH + r, 16), 16), :]
                scale = weight * jnp.minimum(lax.rsqrt(real * real + imag * imag), 1.0 / FLOOR)
                at = pl.ds(pl.multiple_of(i * 16, 16), 16)
                s[0, b, k, at, :] = (weight * real).astype(jnp.bfloat16)
                s[1, b, k, at, :] = (scale * real).astype(jnp.bfloat16)
                s[2, b, k, at, :] = (scale * imag).astype(jnp.bfloat16)
                return 0

            lax.fori_loop(0, CH // 16, stack, 0)

    def rows16(i):
        return pl.ds(pl.multiple_of(i * 16, 16), 16)

    def rows32(i):
        return pl.ds(pl.multiple_of(i * 32, 32), 32)

    def cols512(i):
        return pl.ds(pl.multiple_of(i * 512, 512), 512)

    def cols256(i):
        return pl.ds(pl.multiple_of(i * 256, 256), 256)

    first_a = [
        send(s.at[:, :, 0, rows16(x_peer[d]), :], ra.at[d], x_dev[d]) for d in range(3)
    ]
    first_b = [
        send(s.at[:, lax.rem(y_peer[d], 2), 1, rows32(y_peer[d] // 2), :], rb.at[d], y_dev[d])
        for d in range(3)
    ]
    for copy in first_a:
        copy.wait_recv()
    for v in range(3):
        for b in range(2):
            total = s[v, b, 0, rows16(xx), :].astype(jnp.float32)
            for d in range(3):
                total += ra[d, v, b].astype(jnp.float32)
            pa[v, b] = total.astype(jnp.bfloat16)
    second_a = [
        send(pa.at[:, lax.rem(y_peer[d], 2), :, cols512(y_peer[d] // 2)], ra2.at[d], y_dev[d])
        for d in range(3)
    ]
    for copy in first_b:
        copy.wait_recv()
    for v in range(3):
        total = s[v, ylo, 1, rows32(yhi), :].astype(jnp.float32)
        for d in range(3):
            total += rb[d, v].astype(jnp.float32)
        pb[v] = total.astype(jnp.bfloat16)
    second_b = [
        send(pb.at[:, :, cols256(x_peer[d])], rb2.at[d], x_dev[d]) for d in range(3)
    ]

    def finish(parts):
        linear = parts[0] * (1.0 / 4.0)
        phased = linear * jnp.sqrt(parts[1] * parts[1] + parts[2] * parts[2]) * (1.0 / 16.0)
        return linear.astype(jnp.bfloat16), phased.astype(jnp.bfloat16)

    for copy in second_a:
        copy.wait_recv()
    parts = []
    for v in range(3):
        total = pa[v, ylo, :, cols512(yhi)].astype(jnp.float32)
        for d in range(3):
            total += ra2[d, v].astype(jnp.float32)
        parts.append(total)
    linear, phased = finish(parts)
    g[0, 0, rows16(xx), cols512(yhi)] = linear
    g[1, 0, rows16(xx), cols512(yhi)] = phased
    last = []
    piece = g.at[:, 0, rows16(xx), cols512(yhi)]
    for dev in g_dev:
        last.append(send(piece, piece, dev))
    for copy in second_b:
        copy.wait_recv()
    parts = []
    for v in range(3):
        total = pb[v, :, cols256(xx)].astype(jnp.float32)
        for d in range(3):
            total += rb2[d, v].astype(jnp.float32)
        parts.append(total)
    linear, phased = finish(parts)
    g[0, 1, rows32(yhi), cols256(xx)] = linear
    g[1, 1, rows32(yhi), cols256(xx)] = phased
    piece = g.at[:, 1, rows32(yhi), cols256(xx)]
    for dev in g_dev:
        last.append(send(piece, piece, dev))
    for copy in last:
        copy.wait_recv()

    for k in range(2):
        lin_out[k] = g[0, k].astype(jnp.float32)
        ph_out[k] = g[1, k].astype(jnp.float32)
    bins = jnp.dot(member[0], g[0, 0], preferred_element_type=jnp.float32)
    bins += jnp.dot(member[1], g[0, 1], preferred_element_type=jnp.float32)
    bin_out[...] = bins
    for copy in sent:
        copy.wait_send()


def stacks(wt, offs, keep, member):
    vmem = pl.BlockSpec(memory_space=pltpu.VMEM)
    smem = pl.BlockSpec(memory_space=pltpu.SMEM)
    bf16, f32 = jnp.bfloat16, jnp.float32
    copies = 5 * Q + 3 * Q + 3 * Q + 12 + 14
    block = (12, L, 2, CH, 128)
    return pl.pallas_call(
        kernel,
        out_shape=(
            jax.ShapeDtypeStruct((2, CH, LAGS), f32),
            jax.ShapeDtypeStruct((2, CH, LAGS), f32),
            jax.ShapeDtypeStruct((NBIN, LAGS), f32),
        ),
        in_specs=[pl.BlockSpec(memory_space=pl.ANY), smem, smem, vmem],
        out_specs=(vmem, vmem, vmem),
        scratch_shapes=[
            *[pltpu.VMEM(block, bf16)] * Q,
            pltpu.VMEM((2 * L, 12 * CH, 128), f32),
            pltpu.VMEM((2, F // FINE, LAGS), f32),
            pltpu.VMEM((2, FINE, LAGS), f32),
            pltpu.VMEM((2 * Q, KQ, LAGS), bf16),
            pltpu.VMEM((8 * CH, 2 * KQ), bf16),
            pltpu.VMEM((8 * CH, LAGS), f32),
            pltpu.VMEM((3, 2, 2, CH, LAGS), bf16),
            pltpu.VMEM((3, 3, 2, 16, LAGS), bf16),
            pltpu.VMEM((3, 3, 32, LAGS), bf16),
            pltpu.VMEM((3, 2, 16, LAGS), bf16),
            pltpu.VMEM((3, 32, LAGS), bf16),
            pltpu.VMEM((3, 3, 16, 512), bf16),
            pltpu.VMEM((3, 3, 32, 256), bf16),
            pltpu.VMEM((2, 2, CH, LAGS), bf16),
            pltpu.SemaphoreType.DMA((Q,)),
            pltpu.SemaphoreType.DMA((copies,)),
            pltpu.SemaphoreType.DMA((copies,)),
        ],
        compiler_params=pltpu.CompilerParams(
            collective_id=0, has_side_effects=True, vmem_limit_bytes=48 * 1024 * 1024
        ),
    )(wt, offs, keep, member)


def local(spectra, band_offsets, window_keep, chan_dist):
    win_dev, ch_dev, _, freqs = spectra.shape
    channels = ch_dev * lax.axis_size("chan")
    white = whiten(spectra)
    wt = white.reshape(win_dev, ch_dev, 2, freqs // 128, 128).transpose(0, 3, 2, 1, 4)
    pairs = [(i, i ^ 2) for i in range(lax.axis_size("chan"))]
    offs = jnp.concatenate([band_offsets, lax.ppermute(band_offsets, "chan", pairs)], axis=0)
    own = lax.axis_index("chan") * ch_dev + jnp.arange(ch_dev, dtype=jnp.int32)
    partner = jnp.mod(own[None, :] + band_offsets[0][:, None], channels)
    every = jnp.arange(channels, dtype=jnp.int32)
    own_dist = jnp.sum(jnp.where(own[:, None] == every[None, :], chan_dist[None, :], 0), axis=1)
    partner_dist = jnp.sum(
        jnp.where(partner[:, :, None] == every[None, None, :], chan_dist[None, None, :], 0), axis=2
    )
    bins = jnp.minimum(jnp.abs(partner_dist - own_dist[None, :]), NBIN - 1)
    member = (jnp.arange(NBIN, dtype=jnp.int32)[None, :, None] == bins[:, None, :]).astype(jnp.bfloat16)
    linear, phased, binned = stacks(wt, offs, window_keep, member)
    return (linear.transpose(1, 0, 2), phased.transpose(1, 0, 2), binned)


def solution(mesh):
    in_specs = (P("win", "chan", None, None), P("chan", None), P("win"), P())
    out_specs = (P("chan", None, None), P("chan", None, None), P("chan", None))
    return jax.shard_map(local, mesh=mesh, in_specs=in_specs, out_specs=out_specs, check_vma=False)
```

time: 295 us -> 83.4 us (0.28)
  the two profiles are of different devices: /device:TPU:32 before, /device:TPU:2 now
where the time goes in v1:
time: 83.4 us; the launch traced here: 83 us
  Pallas kernels  67.4 us (81%)
  other arithmetic  9 us (11%)
  local copies, waits for them, and re-layouts  4.19 us (5%)
  starting transfers between devices  1.66 us (2%)
    pallas_call x1, Pallas kernels, stacks(): pl.pallas_call(kernel, out_shape=(jax.ShapeDtypeStruct((2, CH, LAGS), f32...  67.4 us
    unnamed x9, local copies, waits for them, and re-layouts  3.07 us
    reduce_sum x1, other arithmetic, whiten(): power = jnp.mean(values[:, :, 0] ** 2 + values[:, :, 1] ** 2, axis=-1)  2.93 us
    convert_element_type x1, other arithmetic, whiten(): values = spectra.astype(jnp.float32)  2.51 us
  transfers between devices with their start and end apart: 1, of which 0 were waited for; matrix products, arithmetic and copies ran while one was open for 12% of the time, Pallas kernels for 0%

profile of v1, /device:TPU:2, one launch (start us, length us, event | category | flops | bytes accessed | tf_op | source)
XLA Modules:
  0.0 83.0 jit_solution(88346111557488904)
XLA Ops:
  0.6 1.7 %collective-permute-start = (s32[1,2]{1,0:T(1,128)}, s32[1,2]{1,0:T(1,128)S(1)}, u32[]{:S(2)}, u32[]{:S(2)}) collective-permute-start(s32[1,2]{1,0:T(1,128)} %param.5), channel_id=1, source_target_pairs={{0,16},{8,24},{16,0},{24,8},{32,48},{40,56},{48,32},{56,40},{64,80... | collective-permute-start | bytes 32 | tf_op jit(solution)/shard_map/ppermute | solution.py:349
  2.3 0.9 %select_reduce_fusion.1 = s32[64]{0:T(128)S(1)} fusion(s32[2048]{0:T(1024)} %param.7, s32[64]{0:T(128)S(1)} %iota_add_fusion), kind=kLoop, calls=%fused_computation.8 | loop fusion | flops 393152 | bytes 8704 | tf_op jit(solution)/shard_map/reduce_sum | solution.py:353
  3.2 0.7 and_select_fusion
  4.0 1.0 %select_reduce_fusion = s32[2,64]{1,0:T(2,128)S(1)} fusion(s32[2048]{0:T(1024)} %param.7, s32[2,64]{1,0:T(2,128)S(1)} %and_select_fusion), kind=kLoop, calls=%fused_computation.5 | loop fusion | flops 786304 | bytes 9216 | tf_op jit(solution)/shard_map/reduce_sum | solution.py:354
  5.0 0.0 copy-start.1
  5.0 2.5 %convert_element_type.9 = f32[2,64,2,2048]{3,2,1,0:T(2,128)S(1)} convert(bf16[2,64,2,2048]{3,2,1,0:T(2,128)(2,1)} %param.4) | non-fusion elementwise | flops 524288 | bytes 3145728 | tf_op jit(solution)/shard_map/convert_element_type | solution.py:26
  7.5 2.9 %fusion.1 = f32[2,64]{1,0:T(2,128)S(1)} fusion(f32[2,64,2,2048]{3,2,1,0:T(2,128)S(1)} %convert_element_type.9), kind=kLoop, calls=%fused_computation.7 | loop fusion | flops 1048448 | bytes 2097664 | tf_op jit(solution)/shard_map/reduce_sum | solution.py:27
  10.4 0.0 copy-done.1
  10.4 0.9 %multiply_convert_fusion = bf16[2,64,2,2048]{3,2,1,0:T(2,128)(2,1)S(1)} fusion(f32[2,64]{1,0:T(2,128)S(1)} %add_rsqrt_fusion, bf16[2,64,2,2048]{3,2,1,0:T(2,128)(2,1)S(1)} %copy-done.1), kind=kLoop, calls=%fused_computation | loop fusion | flops 1572864 | bytes 2097664 | tf_op jit(solution)/shard_map/convert_element_type | solution.py:28
  11.3 0.0 copy-start.2
  11.3 0.0 copy-start
  11.4 0.7 reshape.86
  12.1 0.4 copy.20
  12.5 0.0 collective-permute-done
  12.5 0.0 copy-done.2
  12.5 0.0 copy-done
  12.5 67.4 %shard_map.67 = (f32[2,64,1024]{2,1,0:T(8,128)S(1)}, f32[2,64,1024]{2,1,0:T(8,128)S(1)}, f32[32,1024]{1,0:T(8,128)S(1)}) custom-call(bf16[2,16,2,64,128]{4,3,2,1,0:T(8,128)(2,1)S(1)} %bitcast.6, s32[2,2]{1,0:T(2,128)S(1)} %pad_add_fusion.offs, s32[2]{0:T(128)S(1)} %copy-done, bf16[2,32,64]{2,1,0:T(8,128)(2,1)S(1)} %fusion.2.member), custom_call_target="tpu_custom_call" | custom-call | tf_op jit(solution)/shard_map/pallas_call | solution.py:308
  80.0 1.2 %copy.15 = f32[64,2,1024]{2,1,0:T(2,128)} copy(f32[64,2,1024]{2,0,1:T(8,128)S(1)} %bitcast.8) | data formatting | bytes 1048576
  81.2 1.2 %copy.16 = f32[64,2,1024]{2,1,0:T(2,128)} copy(f32[64,2,1024]{2,0,1:T(8,128)S(1)} %bitcast.7) | data formatting | bytes 1048576
  82.4 0.7 copy.22
  (5 shorter events, 0.0 us)
Async XLA Ops:
  0.6 11.9 %collective-permute-start = (s32[1,2]{1,0:T(1,128)}, s32[1,2]{1,0:T(1,128)S(1)}, u32[]{:S(2)}, u32[]{:S(2)}) collective-permute-start(s32[1,2]{1,0:T(1,128)} %param.5), channel_id=1, source_target_pairs={{0,16},{8,24},{16,0},{24,8},{32,48},{40,56},{48,32},{56,40},{64,80... | collective-permute-start | bytes 32 | tf_op jit(solution)/shard_map/ppermute | solution.py:349
  5.0 5.5 %copy-start.1 = (bf16[2,64,2,2048]{3,2,1,0:T(2,128)(2,1)S(1)}, bf16[2,64,2,2048]{3,2,1,0:T(2,128)(2,1)}, u32[]{:S(2)}) copy-start(bf16[2,64,2,2048]{3,2,1,0:T(2,128)(2,1)} %param.4) | copy-start | bytes 3145732
  11.3 1.2 %copy-start.2 = (s32[1,2]{1,0:T(1,128)S(1)}, s32[1,2]{1,0:T(1,128)}, u32[]{:S(2)}) copy-start(s32[1,2]{1,0:T(1,128)} %param.5) | copy-start | bytes 28
  11.3 1.2 %copy-start = (s32[2]{0:T(128)S(1)}, s32[2]{0:T(128)}, u32[]{:S(2)}) copy-start(s32[2]{0:T(128)} %keep.1) | copy-start | bytes 28

commit v2 on v1

--- a/solution.py
+++ b/solution.py
@@ -19,13 +19,8 @@
 L = F // 128 // Q
 KQ = L * 128
 FINE = 32
+LIFT = 2.0**20
 MESH = pl.DeviceIdType.MESH
-
-
-def whiten(spectra):
-    values = spectra.astype(jnp.float32)
-    power = jnp.mean(values[:, :, 0] ** 2 + values[:, :, 1] ** 2, axis=-1)
-    return (values * lax.rsqrt(power + EPS)[:, :, None, None]).astype(jnp.bfloat16)
 
 
 def turn(product):
@@ -33,9 +28,9 @@
 
 
 def kernel(
-    wt, offs, keep, member,
+    wt, offs, keep, dist,
     lin_out, ph_out, bin_out,
-    j0, j1, j2, j3, j32, ea, eb, table, x, acc, s,
+    j0, j1, j2, j3, far_offs, j32, power_m, power_o, member, ea, eb, table, x, acc, s,
     ra, rb, pa, pb, ra2, rb2, g,
     local_sem, send_sem, recv_sem,
 ):
@@ -89,6 +84,7 @@
     def near(c):
         return {"chan": c, "win": win}
 
+    offs_copy = send(offs, far_offs, near(across))
     lanes = [pl.ds(q * L, L) for q in range(Q)]
     stay, cross_y, up, down, mate_own = [], [], [], [], []
     for q in range(Q):
@@ -124,6 +120,21 @@
 
     lax.fori_loop(0, F // FINE, fill, 0)
 
+    place = chan * CH + lax.broadcasted_iota(jnp.int32, (CH, 1), 0)
+    every = lax.broadcasted_iota(jnp.int32, (CH, 32 * CH), 1)
+    row_dist = dist[...].astype(jnp.float32)
+
+    def distance(index):
+        return jnp.sum(jnp.where(every == index, row_dist, 0.0), axis=1, keepdims=True)
+
+    own_dist = distance(place)
+    for k in range(2):
+        partner = jnp.bitwise_and(place + offs[0, k], 32 * CH - 1)
+        bins = jnp.minimum(jnp.abs(distance(partner) - own_dist), NBIN - 1.0)
+        column = lax.broadcasted_iota(jnp.int32, (CH, 128), 1).astype(jnp.float32)
+        member[k] = (bins == column).astype(jnp.float32)
+
+    offs_copy.wait_recv()
     up_far, down_far, mate_far = [], [], []
     for q in range(Q):
         cross_y[q].wait_recv()
@@ -143,10 +154,9 @@
     starts = []
     for b in range(2):
         block = core + 2 * b
-        which = jnp.where(block == own, 0, 1)
         for k in range(2):
             starts.append(((4 + block) * CH, (4 + block) * CH + jnp.where(
-                block == own, offs[0, k], offs[1, k])))
+                block == own, offs[0, k], far_offs[0, k])))
 
     for q in range(Q):
         moved = forward(q)
@@ -168,9 +178,16 @@
         for r, (mine_at, other_at) in enumerate(starts):
             at_m = pl.ds(pl.multiple_of(mine_at, CH), CH)
             at_o = pl.ds(other_at, CH)
+            sum_m, sum_o = None, None
             for lg in range(L):
                 mr, mi = j32[lg * 2, at_m, :], j32[lg * 2 + 1, at_m, :]
                 orr, oi = j32[lg * 2, at_o, :], j32[lg * 2 + 1, at_o, :]
+                square = orr * orr + oi * oi
+                sum_o = square if sum_o is None else sum_o + square
+                if r % 2 == 0:
+                    square = mr * mr + mi * mi
+                    sum_m = square if sum_m is None else sum_m + square
+                mr, mi = mr * LIFT, mi * LIFT
                 real = (mr * orr + mi * oi).astype(jnp.bfloat16)
                 imag = (mi * orr - mr * oi).astype(jnp.bfloat16)
                 top = slice(r * CH, (r + 1) * CH)
@@ -181,6 +198,9 @@
                 x[top, two] = -imag
                 x[low, one] = imag
                 x[low, two] = real
+            power_o[r] = sum_o if q == 0 else power_o[r] + sum_o
+            if r % 2 == 0:
+                power_m[r // 2] = sum_m if q == 0 else power_m[r // 2] + sum_m
 
         def multiply(n, _):
             at = pl.ds(pl.multiple_of(n * 256, 256), 256)
@@ -199,10 +219,13 @@
         for k in range(2):
             def stack(i, _):
                 r = (b * 2 + k) * CH + i * 16
-                real = acc[pl.ds(pl.multiple_of(r, 16), 16), :]
-                imag = acc[pl.ds(pl.multiple_of(4 * CH + r, 16), 16), :]
+                at = pl.ds(pl.multiple_of(i * 16, 16), 16)
+                mean_m = jnp.sum(power_m[b, at, :], axis=1, keepdims=True) * (1.0 / F)
+                mean_o = jnp.sum(power_o[b * 2 + k, at, :], axis=1, keepdims=True) * (1.0 / F)
+                gain = lax.rsqrt(mean_m + EPS) * (1.0 / LIFT) * lax.rsqrt(mean_o + EPS)
+                real = acc[pl.ds(pl.multiple_of(r, 16), 16), :] * gain
+                imag = acc[pl.ds(pl.multiple_of(4 * CH + r, 16), 16), :] * gain
                 scale = weight * jnp.minimum(lax.rsqrt(real * real + imag * imag), 1.0 / FLOOR)
-                at = pl.ds(pl.multiple_of(i * 16, 16), 16)
                 s[0, b, k, at, :] = (weight * real).astype(jnp.bfloat16)
                 s[1, b, k, at, :] = (scale * real).astype(jnp.bfloat16)
                 s[2, b, k, at, :] = (scale * imag).astype(jnp.bfloat16)
@@ -292,18 +315,22 @@
     for k in range(2):
         lin_out[k] = g[0, k].astype(jnp.float32)
         ph_out[k] = g[1, k].astype(jnp.float32)
-    bins = jnp.dot(member[0], g[0, 0], preferred_element_type=jnp.float32)
-    bins += jnp.dot(member[1], g[0, 1], preferred_element_type=jnp.float32)
-    bin_out[...] = bins
+    bins = jnp.zeros((128, LAGS), jnp.float32)
+    for k in range(2):
+        bins += lax.dot_general(
+            member[k].astype(jnp.bfloat16), g[0, k], (((0,), (0,)), ((), ())),
+            preferred_element_type=jnp.float32,
+        )
+    bin_out[...] = bins[:NBIN]
     for copy in sent:
         copy.wait_send()
 
 
-def stacks(wt, offs, keep, member):
+def stacks(wt, offs, keep, dist):
     vmem = pl.BlockSpec(memory_space=pltpu.VMEM)
     smem = pl.BlockSpec(memory_space=pltpu.SMEM)
     bf16, f32 = jnp.bfloat16, jnp.float32
-    copies = 5 * Q + 3 * Q + 3 * Q + 12 + 14
+    copies = 1 + 5 * Q + 3 * Q + 3 * Q + 12 + 14
     block = (12, L, 2, CH, 128)
     return pl.pallas_call(
         kernel,
@@ -316,7 +343,11 @@
         out_specs=(vmem, vmem, vmem),
         scratch_shapes=[
             *[pltpu.VMEM(block, bf16)] * Q,
+            pltpu.SMEM((1, 2), jnp.int32),
             pltpu.VMEM((2 * L, 12 * CH, 128), f32),
+            pltpu.VMEM((2, CH, 128), f32),
+            pltpu.VMEM((4, CH, 128), f32),
+            pltpu.VMEM((2, CH, 128), f32),
             pltpu.VMEM((2, F // FINE, LAGS), f32),
             pltpu.VMEM((2, FINE, LAGS), f32),
             pltpu.VMEM((2 * Q, KQ, LAGS), bf16),
@@ -337,26 +368,13 @@
         compiler_params=pltpu.CompilerParams(
             collective_id=0, has_side_effects=True, vmem_limit_bytes=48 * 1024 * 1024
         ),
-    )(wt, offs, keep, member)
+    )(wt, offs, keep, dist)
 
 
 def local(spectra, band_offsets, window_keep, chan_dist):
     win_dev, ch_dev, _, freqs = spectra.shape
-    channels = ch_dev * lax.axis_size("chan")
-    white = whiten(spectra)
-    wt = white.reshape(win_dev, ch_dev, 2, freqs // 128, 128).transpose(0, 3, 2, 1, 4)
-    pairs = [(i, i ^ 2) for i in range(lax.axis_size("chan"))]
-    offs = jnp.concatenate([band_offsets, lax.ppermute(band_offsets, "chan", pairs)], axis=0)
-    own = lax.axis_index("chan") * ch_dev + jnp.arange(ch_dev, dtype=jnp.int32)
-    partner = jnp.mod(own[None, :] + band_offsets[0][:, None], channels)
-    every = jnp.arange(channels, dtype=jnp.int32)
-    own_dist = jnp.sum(jnp.where(own[:, None] == every[None, :], chan_dist[None, :], 0), axis=1)
-    partner_dist = jnp.sum(
-        jnp.where(partner[:, :, None] == every[None, None, :], chan_dist[None, None, :], 0), axis=2
-    )
-    bins = jnp.minimum(jnp.abs(partner_dist - own_dist[None, :]), NBIN - 1)
-    member = (jnp.arange(NBIN, dtype=jnp.int32)[None, :, None] == bins[:, None, :]).astype(jnp.bfloat16)
-    linear, phased, binned = stacks(wt, offs, window_keep, member)
+    wt = spectra.reshape(win_dev, ch_dev, 2, freqs // 128, 128).transpose(0, 3, 2, 1, 4)
+    linear, phased, binned = stacks(wt, band_offsets, window_keep, chan_dist[None, :])
     return (linear.transpose(1, 0, 2), phased.transpose(1, 0, 2), binned)
 
 

time: 83.4 us -> 76.4 us (0.916)
  other arithmetic: 9 us -> 0 us
  Pallas kernels: 67.4 us -> 69.6 us
  local copies, waits for them, and re-layouts: 4.19 us -> 5.86 us
  starting transfers between devices: 1.66 us -> 0 us
    reduce_sum x3 -> x0, other arithmetic: 4.84 us -> none  [the longest x1 2.93 us: whiten(): power = jnp.mean(values[:, :, 0] ** 2 + values[:, :, 1] ** 2, axis=-1)]
    convert_element_type x3 -> x0, other arithmetic: 3.39 us -> none  [the longest x1 2.51 us: whiten(): values = spectra.astype(jnp.float32)]
    pallas_call x1, Pallas kernels: 67.4 us -> 69.6 us  [stacks(): pl.pallas_call(kernel, out_shape=(jax.ShapeDtypeStruct((2, CH, LAGS), f32...]
    ppermute x1 -> x0, starting transfers between devices: 1.66 us -> none  [local(): lax.ppermute(band_offsets, 'chan', pairs)]
    reshape x2, local copies, waits for them, and re-layouts: 1.12 us -> 2.15 us  [local(): spectra.reshape(win_dev, ch_dev, 2, freqs // 128, 128)]
  transfers between devices with their start and end apart: 1 -> 0, of which waited for: 0 -> 0; matrix products, arithmetic and copies ran while one was open for 12% -> 0% of each run, Pallas kernels for 0% -> 0%
where the time goes in v2:
time: 76.4 us; the launch traced here: 76.1 us
  Pallas kernels  69.6 us (91%)
  local copies, waits for them, and re-layouts  5.86 us (8%)
    pallas_call x1, Pallas kernels, stacks(): pl.pallas_call(kernel, out_shape=(jax.ShapeDtypeStruct((2, CH, LAGS), f32...  69.6 us
    unnamed x9, local copies, waits for them, and re-layouts  3.71 us
    reshape x2, local copies, waits for them, and re-layouts, local(): spectra.reshape(win_dev, ch_dev, 2, freqs // 128, 128)  2.15 us

profile of v2, /device:TPU:2, one launch (start us, length us, event | category | flops | bytes accessed | tf_op | source)
XLA Modules:
  0.0 76.1 jit_solution(10028160448932175751)
XLA Ops:
  0.6 1.7 %reshape.10 = bf16[2,64,2,16,128]{4,3,2,1,0:T(8,128)(2,1)S(1)} reshape(bf16[2,64,2,2048]{3,2,1,0:T(2,128)(2,1)} %param.4) | data formatting | bytes 2097152 | tf_op jit(solution)/shard_map/reshape | solution.py:376
  2.4 0.0 copy-start
  2.4 0.4 copy.16
  2.8 0.0 copy-start.1
  2.8 0.0 copy-start.2
  2.8 0.2 copy-done
  3.1 0.4 copy-done.1
  3.5 0.0 copy-done.2
  3.5 69.6 %shard_map.67 = (f32[2,64,1024]{2,1,0:T(8,128)S(1)}, f32[2,64,1024]{2,1,0:T(8,128)S(1)}, f32[32,1024]{1,0:T(8,128)S(1)}) custom-call(bf16[2,16,2,64,128]{4,3,2,1,0:T(8,128)(2,1)S(1)} %bitcast.6, s32[1,2]{1,0:T(1,128)S(1)} %copy-done.1, s32[2]{0:T(128)S(1)} %copy-done.2, s32[1,2048]{1,0:T(1,128)S(1)} %bitcast.9), custom_call_target="tpu_custom_call" | custom-call | tf_op jit(solution)/shard_map/pallas_call | solution.py:335
  73.1 1.2 %copy.11 = f32[64,2,1024]{2,1,0:T(2,128)} copy(f32[64,2,1024]{2,0,1:T(8,128)S(1)} %bitcast.8) | data formatting | bytes 1048576
  74.3 1.2 %copy.12 = f32[64,2,1024]{2,1,0:T(2,128)} copy(f32[64,2,1024]{2,0,1:T(8,128)S(1)} %bitcast.7) | data formatting | bytes 1048576
  75.5 0.7 copy.18
Async XLA Ops:
  2.4 0.7 copy-start
  2.8 0.7 copy-start.1
  2.8 0.7 copy-start.2

commit v3 on v2

v3 whole, which is shorter than its diff:
```python
import functools
import math

import jax
import jax.numpy as jnp
from jax import lax
from jax.experimental import pallas as pl
from jax.experimental.pallas import tpu as pltpu
from jax.sharding import PartitionSpec as P

LAGS = 1024
NBIN = 32
EPS = 1e-06
FLOOR = 0.1

F = 2048
CH = 64
Q = 4
L = F // 128 // Q
KQ = L * 128
FINE = 32
LIFT = 2.0**20
MESH = pl.DeviceIdType.MESH


def turn(product):
    return jnp.bitwise_and(product, 2 * F - 1).astype(jnp.float32) * (math.pi / F)


def kernel(
    wt, offs, keep, dist,
    lin_out, ph_out, bin_out,
    j0, j1, j2, j3, far_offs, j32, power_m, power_o, member, ea, eb, table, x, acc,
    s_early, s_late, ra_early, ra_late, pa_early, pa_late, rb, pb, ra2, rb2, g,
    local_sem, send_sem, recv_sem,
):
    joined = (j0, j1, j2, j3)
    chan = lax.axis_index("chan")
    win = lax.axis_index("win")
    core = lax.rem(chan, 2)
    ylo = lax.rem(chan // 2, 2)
    xx = win // 2
    yhi = lax.rem(win, 2)
    above = lax.rem(chan + 4, 32)
    below = lax.rem(chan + 28, 32)
    mate = chan + 1 - 2 * core
    across = chan + 2 - 4 * ylo
    own = ylo * 2 + core
    far = (1 - ylo) * 2 + core
    first_way = jnp.where(ylo == 1, above, below)
    other_way = jnp.where(ylo == 1, below, above)
    early_way = jnp.where(core == 0, below, above)
    late_way = jnp.where(core == 0, above, below)
    early = 2 - core
    late = 3 * core
    owns_early = ylo + core == 1
    owns_late = ylo == core

    x_peer = [lax.rem(xx + d, 4) for d in (1, 2, 3)]
    x_dev = [{"chan": chan, "win": p * 2 + yhi} for p in x_peer]
    y_dev = [
        {"chan": chan, "win": win + 1 - 2 * yhi},
        {"chan": across, "win": win},
        {"chan": across, "win": win + 1 - 2 * yhi},
    ]
    y_half = [1 - yhi, yhi, 1 - yhi]
    far_x = [{"chan": chan, "win": p * 2 + 1 - yhi} for p in x_peer]
    g_dev = [y_dev[0]] + x_dev + far_x

    barrier = pltpu.get_barrier_semaphore()
    greet = [{"chan": c, "win": win} for c in (above, below, mate)] + y_dev + x_dev + far_x
    for dev in greet:
        pl.semaphore_signal(barrier, inc=1, device_id=dev, device_id_type=MESH)
    pl.semaphore_wait(barrier, len(greet))

    count = [0]
    sent = []

    def make(src, dst, device, when=None):
        i = count[0]
        count[0] += 1
        copy = pltpu.make_async_remote_copy(
            src_ref=src, dst_ref=dst, send_sem=send_sem.at[i], recv_sem=recv_sem.at[i],
            device_id=device, device_id_type=MESH,
        )
        sent.append((when, copy))
        return copy

    def send(*args, **kwargs):
        copy = make(*args, **kwargs)
        copy.start()
        return copy

    def near(c):
        return {"chan": c, "win": win}

    offs_copy = send(offs, far_offs, near(across))
    lanes = [pl.ds(q * L, L) for q in range(Q)]
    stay, cross_y, own_first, mate_own = [], [], [], []
    for q in range(Q):
        mine = wt.at[ylo, lanes[q]]
        copy = pltpu.make_async_copy(mine, joined[q].at[4 + own], local_sem.at[q])
        copy.start()
        stay.append(copy)
        cross_y.append(send(wt.at[1 - ylo, lanes[q]], joined[q].at[4 + own], near(across)))
        own_first.append(send(mine, joined[q].at[8 + core - 6 * ylo], near(first_way)))
        mate_own.append(send(mine, joined[q].at[4 + own], near(mate)))
    for_early = [
        make(joined[q].at[4 + early], joined[q].at[10 - 9 * core], near(early_way)) for q in range(Q)
    ]
    for_late = [
        make(joined[q].at[4 + late], joined[q].at[11 * core], near(late_way)) for q in range(Q)
    ]
    for copy in stay:
        copy.wait()

    @pl.when(owns_early)
    def _():
        for_early[0].start()

    @pl.when(owns_late)
    def _():
        for_late[0].start()

    lag = lax.broadcasted_iota(jnp.int32, (FINE, LAGS), 1) - LAGS // 2
    row = lax.broadcasted_iota(jnp.int32, (FINE, LAGS), 0)
    fine = turn(row * lag)
    eb[0] = jnp.cos(fine) * (1.0 / math.sqrt(F))
    eb[1] = jnp.sin(fine) * (1.0 / math.sqrt(F))
    for half in range(F // FINE // FINE):
        coarse = turn((row + half * FINE) * FINE * lag)
        ea[0, half * FINE:(half + 1) * FINE] = jnp.cos(coarse)
        ea[1, half * FINE:(half + 1) * FINE] = jnp.sin(coarse)

    per = KQ // FINE

    def fill(a, _):
        ca = ea[0, pl.ds(a, 1), :]
        sa = ea[1, pl.ds(a, 1), :]
        q2 = (a // per) * 2
        at = pl.ds(pl.multiple_of(lax.rem(a, per) * FINE, FINE), FINE)
        table[q2, at, :] = (eb[0] * ca - eb[1] * sa).astype(jnp.bfloat16)
        table[q2 + 1, at, :] = (eb[1] * ca + eb[0] * sa).astype(jnp.bfloat16)
        return 0

    far_first, mate_far = [], []
    for q in range(Q):
        cross_y[q].wait_recv()
        mine = joined[q].at[4 + far]
        far_first.append(send(mine, joined[q].at[2 + core + 6 * ylo], near(other_way)))
        mate_far.append(send(mine, joined[q].at[4 + far], near(mate)))
        lax.fori_loop(q * per, (q + 1) * per, fill, 0)

    @pl.when(owns_late)
    def _():
        for_early[0].start()

    for q in range(1, Q):
        for_early[q].start()

    place = chan * CH + lax.broadcasted_iota(jnp.int32, (CH, 1), 0)
    every = lax.broadcasted_iota(jnp.int32, (CH, 32 * CH), 1)
    row_dist = dist[...].astype(jnp.float32)

    def distance(index):
        return jnp.sum(jnp.where(every == index, row_dist, 0.0), axis=1, keepdims=True)

    own_dist = distance(place)
    for k in range(2):
        partner = jnp.bitwise_and(place + offs[0, k], 32 * CH - 1)
        bins = jnp.minimum(jnp.abs(distance(partner) - own_dist), NBIN - 1.0)
        column = lax.broadcasted_iota(jnp.int32, (CH, 128), 1).astype(jnp.float32)
        member[k] = (bins == column).astype(jnp.float32)

    offs_copy.wait_recv()
    forward = []
    for q in range(Q):
        own_first[q].wait_recv()
        far_first[q].wait_recv()
        forward.append([
            send(joined[q].at[pos], joined[q].at[pos], near(mate)) for pos in (2 + core, 8 + core)
        ])

    def widen(q, first, number):
        def one(i, _):
            p = first + i
            at = pl.ds(pl.multiple_of(p * CH, CH), CH)
            for lg in range(L):
                for ri in range(2):
                    j32[(q * L + lg) * 2 + ri, at, :] = joined[q][p, lg, ri].astype(jnp.float32)
            return 0

        lax.fori_loop(0, number, one, 0)

    def correlate(q, h, block, owns):
        at_m = pl.ds(pl.multiple_of((4 + block) * CH, CH), CH)
        for k in range(2):
            at_o = pl.ds((4 + block) * CH + jnp.where(owns, offs[0, k], far_offs[0, k]), CH)
            sum_m, sum_o = None, None
            for lg in range(L):
                j = (q * L + lg) * 2
                mr, mi = j32[j, at_m, :], j32[j + 1, at_m, :]
                orr, oi = j32[j, at_o, :], j32[j + 1, at_o, :]
                square = orr * orr + oi * oi
                sum_o = square if sum_o is None else sum_o + square
                if k == 0:
                    square = mr * mr + mi * mi
                    sum_m = square if sum_m is None else sum_m + square
                mr, mi = mr * LIFT, mi * LIFT
                real = (mr * orr + mi * oi).astype(jnp.bfloat16)
                imag = (mi * orr - mr * oi).astype(jnp.bfloat16)
                top = slice(k * CH, (k + 1) * CH)
                low = slice((2 + k) * CH, (3 + k) * CH)
                one = slice(lg * 128, (lg + 1) * 128)
                two = slice(KQ + lg * 128, KQ + (lg + 1) * 128)
                x[top, one] = real
                x[top, two] = -imag
                x[low, one] = imag
                x[low, two] = real
            power_o[h * 2 + k] = sum_o if q == 0 else power_o[h * 2 + k] + sum_o
            if k == 0:
                power_m[h] = sum_m if q == 0 else power_m[h] + sum_m

        def multiply(n, _):
            at = pl.ds(pl.multiple_of(n * 256, 256), 256)
            value = jnp.dot(x[:, :KQ], table[2 * q, :, at], preferred_element_type=jnp.float32)
            value += jnp.dot(x[:, KQ:], table[2 * q + 1, :, at], preferred_element_type=jnp.float32)
            if q == 0:
                acc[:, at] = value
            else:
                acc[:, at] += value
            return 0

        lax.fori_loop(0, LAGS // 256, multiply, 0)

    weight = jnp.where(ylo == 0, keep[0], keep[1]).astype(jnp.float32)

    def stack(h, s):
        for k in range(2):
            def one(i, _):
                r = k * CH + i * 16
                at = pl.ds(pl.multiple_of(i * 16, 16), 16)
                mean_m = jnp.sum(power_m[h, at, :], axis=1, keepdims=True) * (1.0 / F)
                mean_o = jnp.sum(power_o[h * 2 + k, at, :], axis=1, keepdims=True) * (1.0 / F)
                gain = lax.rsqrt(mean_m + EPS) * (1.0 / LIFT) * lax.rsqrt(mean_o + EPS)
                real = acc[pl.ds(pl.multiple_of(r, 16), 16), :] * gain
                imag = acc[pl.ds(pl.multiple_of(2 * CH + r, 16), 16), :] * gain
                scale = weight * jnp.minimum(lax.rsqrt(real * real + imag * imag), 1.0 / FLOOR)
                s[0, k, at, :] = (weight * real).astype(jnp.bfloat16)
                s[1, k, at, :] = (scale * real).astype(jnp.bfloat16)
                s[2, k, at, :] = (scale * imag).astype(jnp.bfloat16)
                return 0

            lax.fori_loop(0, CH // 16, one, 0)

    def rows16(i):
        return pl.ds(pl.multiple_of(i * 16, 16), 16)

    def rows32(i):
        return pl.ds(pl.multiple_of(i * 32, 32), 32)

    def cols512(i):
        return pl.ds(pl.multiple_of(i * 512, 512), 512)

    def cols256(i):
        return pl.ds(pl.multiple_of(i * 256, 256), 256)

    def to_owners(source, target, owns):
        copies = [
            make(source(y_half[n]), target.at[n], y_dev[n], when=owns if n == 0 else ~owns)
            for n in range(3)
        ]

        @pl.when(owns)
        def _():
            copies[0].start()

        @pl.when(~owns)
        def _():
            copies[1].start()
            copies[2].start()

        return copies

    def first_sums(s, ra, owns):
        a = [send(s.at[:, 0, rows16(x_peer[d]), :], ra.at[d], x_dev[d]) for d in range(3)]
        b = to_owners(lambda half: s.at[:, 1, rows32(half), :], rb, owns)
        return a, b

    def second_sums(s, ra, pa, owns, copies):
        a, b = copies
        for copy in a:
            copy.wait_recv()
        for v in range(3):
            total = s[v, 0, rows16(xx), :].astype(jnp.float32)
            for d in range(3):
                total += ra[d, v].astype(jnp.float32)
            pa[v] = total.astype(jnp.bfloat16)
        a2 = to_owners(lambda half: pa.at[:, :, cols512(half)], ra2, owns)
        b2 = [make(pb.at[:, :, cols256(x_peer[d])], rb2.at[d], x_dev[d], when=owns) for d in range(3)]

        @pl.when(owns)
        def _():
            for copy in b:
                copy.wait_recv()
            for v in range(3):
                total = s[v, 1, rows32(yhi), :].astype(jnp.float32)
                for d in range(3):
                    total += rb[d, v].astype(jnp.float32)
                pb[v] = total.astype(jnp.bfloat16)
            for copy in b2:
                copy.start()

        return a2, b2

    def finish(parts):
        linear = parts[0] * (1.0 / 4.0)
        phased = linear * jnp.sqrt(parts[1] * parts[1] + parts[2] * parts[2]) * (1.0 / 16.0)
        return linear.astype(jnp.bfloat16), phased.astype(jnp.bfloat16)

    piece_a = g.at[:, 0, rows16(xx), cols512(yhi)]
    piece_b = g.at[:, 1, rows32(yhi), cols256(xx)]
    last_a = [make(piece_a, piece_a, dev) for dev in g_dev]
    last_b = [make(piece_b, piece_b, dev) for dev in g_dev]

    def results(pa, owns, copies):
        a2, b2 = copies

        @pl.when(owns)
        def _():
            for copy in a2:
                copy.wait_recv()
            parts = []
            for v in range(3):
                total = pa[v, :, cols512(yhi)].astype(jnp.float32)
                for d in range(3):
                    total += ra2[d, v].astype(jnp.float32)
                parts.append(total)
            linear, phased = finish(parts)
            g[0, 0, rows16(xx), cols512(yhi)] = linear
            g[1, 0, rows16(xx), cols512(yhi)] = phased
            for copy in last_a:
                copy.start()
            for copy in b2:
                copy.wait_recv()
            parts = []
            for v in range(3):
                total = pb[v, :, cols256(xx)].astype(jnp.float32)
                for d in range(3):
                    total += rb2[d, v].astype(jnp.float32)
                parts.append(total)
            linear, phased = finish(parts)
            g[0, 1, rows32(yhi), cols256(xx)] = linear
            g[1, 1, rows32(yhi), cols256(xx)] = phased
            for copy in last_b:
                copy.start()

    pass_on = []
    for q in range(Q):
        mate_own[q].wait_recv()
        mate_far[q].wait_recv()
        for copy in forward[q]:
            copy.wait_recv()
        for_early[q].wait_recv()
        pos = 10 - 9 * core
        pass_on.append(send(joined[q].at[pos], joined[q].at[pos], near(mate)))
        if q == 0:
            @pl.when(owns_early)
            def _():
                for_late[0].start()
        else:
            for_late[q].start()
        widen(q, 2 - core, 9)
        correlate(q, 0, early, owns_early)
    stack(0, s_early)
    early_first = first_sums(s_early, ra_early, owns_early)
    for q in range(Q):
        pass_on[q].wait_recv()
        for_late[q].wait_recv()
        widen(q, 10 * core, 2)
        correlate(q, 1, late, owns_late)
        if q == 1:
            early_second = second_sums(s_early, ra_early, pa_early, owns_early, early_first)
    stack(1, s_late)
    late_first = first_sums(s_late, ra_late, owns_late)
    results(pa_early, owns_early, early_second)
    late_second = second_sums(s_late, ra_late, pa_late, owns_late, late_first)
    results(pa_late, owns_late, late_second)

    for copy in last_a + last_b:
        copy.wait_recv()
    for k in range(2):
        lin_out[k] = g[0, k].astype(jnp.float32)
        ph_out[k] = g[1, k].astype(jnp.float32)
    bins = jnp.zeros((128, LAGS), jnp.float32)
    for k in range(2):
        bins += lax.dot_general(
            member[k].astype(jnp.bfloat16), g[0, k], (((0,), (0,)), ((), ())),
            preferred_element_type=jnp.float32,
        )
    bin_out[...] = bins[:NBIN]
    for when, copy in sent:
        if when is None:
            copy.wait_send()
        else:
            pl.when(when)(copy.wait_send)


def stacks(wt, offs, keep, dist):
    vmem = pl.BlockSpec(memory_space=pltpu.VMEM)
    smem = pl.BlockSpec(memory_space=pltpu.SMEM)
    bf16, f32 = jnp.bfloat16, jnp.float32
    copies = 1 + 10 * Q + 2 * 12 + 14
    block = (12, L, 2, CH, 128)
    return pl.pallas_call(
        kernel,
        out_shape=(
            jax.ShapeDtypeStruct((2, CH, LAGS), f32),
            jax.ShapeDtypeStruct((2, CH, LAGS), f32),
            jax.ShapeDtypeStruct((NBIN, LAGS), f32),
        ),
        in_specs=[pl.BlockSpec(memory_space=pl.ANY), smem, smem, vmem],
        out_specs=(vmem, vmem, vmem),
        scratch_shapes=[
            *[pltpu.VMEM(block, bf16)] * Q,
            pltpu.SMEM((1, 2), jnp.int32),
            pltpu.VMEM((Q * 2 * L, 12 * CH, 128), f32),
            pltpu.VMEM((2, CH, 128), f32),
            pltpu.VMEM((4, CH, 128), f32),
            pltpu.VMEM((2, CH, 128), f32),
            pltpu.VMEM((2, F // FINE, LAGS), f32),
            pltpu.VMEM((2, FINE, LAGS), f32),
            pltpu.VMEM((2 * Q, KQ, LAGS), bf16),
            pltpu.VMEM((4 * CH, 2 * KQ), bf16),
            pltpu.VMEM((4 * CH, LAGS), f32),
            pltpu.VMEM((3, 2, CH, LAGS), bf16),
            pltpu.VMEM((3, 2, CH, LAGS), bf16),
            pltpu.VMEM((3, 3, 16, LAGS), bf16),
            pltpu.VMEM((3, 3, 16, LAGS), bf16),
            pltpu.VMEM((3, 16, LAGS), bf16),
            pltpu.VMEM((3, 16, LAGS), bf16),
            pltpu.VMEM((3, 3, 32, LAGS), bf16),
            pltpu.VMEM((3, 32, LAGS), bf16),
            pltpu.VMEM((3, 3, 16, 512), bf16),
            pltpu.VMEM((3, 3, 32, 256), bf16),
            pltpu.VMEM((2, 2, CH, LAGS), bf16),
            pltpu.SemaphoreType.DMA((Q,)),
            pltpu.SemaphoreType.DMA((copies,)),
            pltpu.SemaphoreType.DMA((copies,)),
        ],
        compiler_params=pltpu.CompilerParams(
            collective_id=0, has_side_effects=True, vmem_limit_bytes=52 * 1024 * 1024
        ),
    )(wt, offs, keep, dist)


def local(spectra, band_offsets, window_keep, chan_dist):
    win_dev, ch_dev, _, freqs = spectra.shape
    wt = spectra.reshape(win_dev, ch_dev, 2, freqs // 128, 128).transpose(0, 3, 2, 1, 4)
    linear, phased, binned = stacks(wt, band_offsets, window_keep, chan_dist[None, :])
    return (linear.transpose(1, 0, 2), phased.transpose(1, 0, 2), binned)


def solution(mesh):
    in_specs = (P("win", "chan", None, None), P("chan", None), P("win"), P())
    out_specs = (P("chan", None, None), P("chan", None, None), P("chan", None))
    return jax.shard_map(local, mesh=mesh, in_specs=in_specs, out_specs=out_specs, check_vma=False)
```

time: 76.4 us -> 78.8 us (1.031)
  the two profiles are of different devices: /device:TPU:2 before, /device:TPU:96 now
where the time goes in v3:
time: 78.8 us; the launch traced here: 78.7 us
  Pallas kernels  71.2 us (90%)
  local copies, waits for them, and re-layouts  6.84 us (9%)
    pallas_call x1, Pallas kernels, stacks(): pl.pallas_call(kernel, out_shape=(jax.ShapeDtypeStruct((2, CH, LAGS), f32...  71.2 us
    unnamed x9, local copies, waits for them, and re-layouts  3.72 us
    reshape x2, local copies, waits for them, and re-layouts, local(): spectra.reshape(win_dev, ch_dev, 2, freqs // 128, 128)  3.12 us

profile of v3, /device:TPU:96, one launch (start us, length us, event | category | flops | bytes accessed | tf_op | source)
XLA Modules:
  0.0 78.7 jit_solution(5907169225853836275)
XLA Ops:
  0.6 1.7 %reshape.10 = bf16[2,64,2,16,128]{4,3,2,1,0:T(8,128)(2,1)S(1)} reshape(bf16[2,64,2,2048]{3,2,1,0:T(2,128)(2,1)} %param.4) | data formatting | bytes 2097152 | tf_op jit(solution)/shard_map/reshape | solution.py:459
  2.4 0.0 copy-start
  2.4 1.4 %copy.16 = bf16[2,64,2,16,128]{4,1,2,3,0:T(8,128)(2,1)} copy(bf16[2,64,2,16,128]{4,3,2,1,0:T(8,128)(2,1)S(1)} %reshape.10) | data formatting | bytes 2097152 | tf_op jit(solution)/shard_map/reshape | solution.py:459
  3.8 0.0 copy-start.1
  3.8 0.0 copy-start.2
  3.8 0.0 copy-done
  3.8 0.6 copy-done.1
  4.4 0.0 copy-done.2
  4.4 71.2 %shard_map.67 = (f32[2,64,1024]{2,1,0:T(8,128)S(1)}, f32[2,64,1024]{2,1,0:T(8,128)S(1)}, f32[32,1024]{1,0:T(8,128)S(1)}) custom-call(bf16[2,16,2,64,128]{4,3,2,1,0:T(8,128)(2,1)} %bitcast.9, s32[1,2]{1,0:T(1,128)S(1)} %copy-done.1, s32[2]{0:T(128)S(1)} %copy-done.2, s32[1,2048]{1,0:T(1,128)S(1)} %bitcast.8), custom_call_target="tpu_custom_call" | custom-call | tf_op jit(solution)/shard_map/pallas_call | solution.py:415
  75.6 1.2 %copy.11 = f32[64,2,1024]{2,1,0:T(2,128)} copy(f32[64,2,1024]{2,0,1:T(8,128)S(1)} %bitcast.7) | data formatting | bytes 1048576
  76.8 1.2 %copy.12 = f32[64,2,1024]{2,1,0:T(2,128)} copy(f32[64,2,1024]{2,0,1:T(8,128)S(1)} %bitcast.6) | data formatting | bytes 1048576
  78.0 0.7 copy.18
Async XLA Ops:
  2.4 1.4 %copy-start = (s32[2048]{0:T(1024)S(1)}, s32[2048]{0:T(1024)}, u32[]{:S(2)}) copy-start(s32[2048]{0:T(1024)} %param.7) | copy-start | bytes 24580
  3.8 0.7 copy-start.1
  3.8 0.7 copy-start.2

commit v4 on v3

--- a/solution.py
+++ b/solution.py
@@ -379,12 +379,11 @@
         for_late[q].wait_recv()
         widen(q, 10 * core, 2)
         correlate(q, 1, late, owns_late)
-        if q == 1:
-            early_second = second_sums(s_early, ra_early, pa_early, owns_early, early_first)
     stack(1, s_late)
     late_first = first_sums(s_late, ra_late, owns_late)
+    early_second = second_sums(s_early, ra_early, pa_early, owns_early, early_first)
+    late_second = second_sums(s_late, ra_late, pa_late, owns_late, late_first)
     results(pa_early, owns_early, early_second)
-    late_second = second_sums(s_late, ra_late, pa_late, owns_late, late_first)
     results(pa_late, owns_late, late_second)
 
     for copy in last_a + last_b:

time: 78.8 us -> 71.4 us (0.906)
  the two profiles are of different devices: /device:TPU:96 before, /device:TPU:2 now
where the time goes in v4:
time: 71.4 us; the launch traced here: 71.2 us
  Pallas kernels  63.7 us (89%)
  local copies, waits for them, and re-layouts  6.84 us (10%)
    pallas_call x1, Pallas kernels, stacks(): pl.pallas_call(kernel, out_shape=(jax.ShapeDtypeStruct((2, CH, LAGS), f32...  63.7 us
    unnamed x9, local copies, waits for them, and re-layouts  3.72 us
    reshape x2, local copies, waits for them, and re-layouts, local(): spectra.reshape(win_dev, ch_dev, 2, freqs // 128, 128)  3.12 us

profile of v4, /device:TPU:2, one launch (start us, length us, event | category | flops | bytes accessed | tf_op | source)
XLA Modules:
  0.0 71.2 jit_solution(6299217955403434061)
XLA Ops:
  0.6 1.7 %reshape.10 = bf16[2,64,2,16,128]{4,3,2,1,0:T(8,128)(2,1)S(1)} reshape(bf16[2,64,2,2048]{3,2,1,0:T(2,128)(2,1)} %param.4) | data formatting | bytes 2097152 | tf_op jit(solution)/shard_map/reshape | solution.py:458
  2.4 0.0 copy-start
  2.4 1.4 %copy.16 = bf16[2,64,2,16,128]{4,1,2,3,0:T(8,128)(2,1)} copy(bf16[2,64,2,16,128]{4,3,2,1,0:T(8,128)(2,1)S(1)} %reshape.10) | data formatting | bytes 2097152 | tf_op jit(solution)/shard_map/reshape | solution.py:458
  3.8 0.0 copy-start.1
  3.8 0.0 copy-start.2
  3.8 0.0 copy-done
  3.8 0.6 copy-done.1
  4.4 0.0 copy-done.2
  4.4 63.7 %shard_map.67 = (f32[2,64,1024]{2,1,0:T(8,128)S(1)}, f32[2,64,1024]{2,1,0:T(8,128)S(1)}, f32[32,1024]{1,0:T(8,128)S(1)}) custom-call(bf16[2,16,2,64,128]{4,3,2,1,0:T(8,128)(2,1)} %bitcast.9, s32[1,2]{1,0:T(1,128)S(1)} %copy-done.1, s32[2]{0:T(128)S(1)} %copy-done.2, s32[1,2048]{1,0:T(1,128)S(1)} %bitcast.8), custom_call_target="tpu_custom_call" | custom-call | tf_op jit(solution)/shard_map/pallas_call | solution.py:414
  68.2 1.2 %copy.11 = f32[64,2,1024]{2,1,0:T(2,128)} copy(f32[64,2,1024]{2,0,1:T(8,128)S(1)} %bitcast.7) | data formatting | bytes 1048576
  69.4 1.2 %copy.12 = f32[64,2,1024]{2,1,0:T(2,128)} copy(f32[64,2,1024]{2,0,1:T(8,128)S(1)} %bitcast.6) | data formatting | bytes 1048576
  70.6 0.7 copy.18
Async XLA Ops:
  2.4 1.4 %copy-start = (s32[2048]{0:T(1024)S(1)}, s32[2048]{0:T(1024)}, u32[]{:S(2)}) copy-start(s32[2048]{0:T(1024)} %param.7) | copy-start | bytes 24580
  3.8 0.7 copy-start.1
  3.8 0.7 copy-start.2

commit v5 on v4

--- a/solution.py
+++ b/solution.py
@@ -28,11 +28,11 @@
 
 
 def kernel(
-    wt, offs, keep, dist,
+    wt, offs_in, keep_in, dist_in,
     lin_out, ph_out, bin_out,
-    j0, j1, j2, j3, far_offs, j32, power_m, power_o, member, ea, eb, table, x, acc,
+    j0, j1, j2, j3, offs, keep, dist, far_offs, j32, power_m, power_o, member, ea, eb, table, x, acc,
     s_early, s_late, ra_early, ra_late, pa_early, pa_late, rb, pb, ra2, rb2, g,
-    local_sem, send_sem, recv_sem,
+    local_sem, small_sem, send_sem, recv_sem,
 ):
     joined = (j0, j1, j2, j3)
     chan = lax.axis_index("chan")
@@ -67,6 +67,12 @@
     far_x = [{"chan": chan, "win": p * 2 + 1 - yhi} for p in x_peer]
     g_dev = [y_dev[0]] + x_dev + far_x
 
+    small = [
+        pltpu.make_async_copy(source, target, small_sem.at[n])
+        for n, (source, target) in enumerate(((offs_in, offs), (keep_in, keep), (dist_in, dist)))
+    ]
+    for copy in small:
+        copy.start()
     barrier = pltpu.get_barrier_semaphore()
     greet = [{"chan": c, "win": win} for c in (above, below, mate)] + y_dev + x_dev + far_x
     for dev in greet:
@@ -94,15 +100,14 @@
     def near(c):
         return {"chan": c, "win": win}
 
-    offs_copy = send(offs, far_offs, near(across))
-    lanes = [pl.ds(q * L, L) for q in range(Q)]
+    lanes = [pl.ds(q * KQ, KQ) for q in range(Q)]
     stay, cross_y, own_first, mate_own = [], [], [], []
     for q in range(Q):
-        mine = wt.at[ylo, lanes[q]]
+        mine = wt.at[ylo, :, :, lanes[q]]
         copy = pltpu.make_async_copy(mine, joined[q].at[4 + own], local_sem.at[q])
         copy.start()
         stay.append(copy)
-        cross_y.append(send(wt.at[1 - ylo, lanes[q]], joined[q].at[4 + own], near(across)))
+        cross_y.append(send(wt.at[1 - ylo, :, :, lanes[q]], joined[q].at[4 + own], near(across)))
         own_first.append(send(mine, joined[q].at[8 + core - 6 * ylo], near(first_way)))
         mate_own.append(send(mine, joined[q].at[4 + own], near(mate)))
     for_early = [
@@ -111,16 +116,14 @@
     for_late = [
         make(joined[q].at[4 + late], joined[q].at[11 * core], near(late_way)) for q in range(Q)
     ]
-    for copy in stay:
+    for copy in small + stay:
         copy.wait()
+    offs_copy = send(offs, far_offs, near(across))
 
     @pl.when(owns_early)
     def _():
         for_early[0].start()
-
-    @pl.when(owns_late)
-    def _():
-        for_late[0].start()
+        for_early[1].start()
 
     lag = lax.broadcasted_iota(jnp.int32, (FINE, LAGS), 1) - LAGS // 2
     row = lax.broadcasted_iota(jnp.int32, (FINE, LAGS), 0)
@@ -149,13 +152,11 @@
         mine = joined[q].at[4 + far]
         far_first.append(send(mine, joined[q].at[2 + core + 6 * ylo], near(other_way)))
         mate_far.append(send(mine, joined[q].at[4 + far], near(mate)))
+        if q >= 2:
+            pl.when(owns_late)(for_early[q - 2].start)
         lax.fori_loop(q * per, (q + 1) * per, fill, 0)
 
-    @pl.when(owns_late)
-    def _():
-        for_early[0].start()
-
-    for q in range(1, Q):
+    for q in range(2, Q):
         for_early[q].start()
 
     place = chan * CH + lax.broadcasted_iota(jnp.int32, (CH, 1), 0)
@@ -187,7 +188,7 @@
             at = pl.ds(pl.multiple_of(p * CH, CH), CH)
             for lg in range(L):
                 for ri in range(2):
-                    j32[(q * L + lg) * 2 + ri, at, :] = joined[q][p, lg, ri].astype(jnp.float32)
+                    j32[(q * L + lg) * 2 + ri, at, :] = joined[q][p, ri, :, lg * 128:(lg + 1) * 128].astype(jnp.float32)
             return 0
 
         lax.fori_loop(0, number, one, 0)
@@ -364,12 +365,7 @@
         for_early[q].wait_recv()
         pos = 10 - 9 * core
         pass_on.append(send(joined[q].at[pos], joined[q].at[pos], near(mate)))
-        if q == 0:
-            @pl.when(owns_early)
-            def _():
-                for_late[0].start()
-        else:
-            for_late[q].start()
+        for_late[q].start()
         widen(q, 2 - core, 9)
         correlate(q, 0, early, owns_early)
     stack(0, s_early)
@@ -389,8 +385,8 @@
     for copy in last_a + last_b:
         copy.wait_recv()
     for k in range(2):
-        lin_out[k] = g[0, k].astype(jnp.float32)
-        ph_out[k] = g[1, k].astype(jnp.float32)
+        lin_out[:, k, :] = g[0, k].astype(jnp.float32)
+        ph_out[:, k, :] = g[1, k].astype(jnp.float32)
     bins = jnp.zeros((128, LAGS), jnp.float32)
     for k in range(2):
         bins += lax.dot_general(
@@ -407,21 +403,23 @@
 
 def stacks(wt, offs, keep, dist):
     vmem = pl.BlockSpec(memory_space=pltpu.VMEM)
-    smem = pl.BlockSpec(memory_space=pltpu.SMEM)
     bf16, f32 = jnp.bfloat16, jnp.float32
     copies = 1 + 10 * Q + 2 * 12 + 14
-    block = (12, L, 2, CH, 128)
+    block = (12, 2, CH, KQ)
     return pl.pallas_call(
         kernel,
         out_shape=(
-            jax.ShapeDtypeStruct((2, CH, LAGS), f32),
-            jax.ShapeDtypeStruct((2, CH, LAGS), f32),
+            jax.ShapeDtypeStruct((CH, 2, LAGS), f32),
+            jax.ShapeDtypeStruct((CH, 2, LAGS), f32),
             jax.ShapeDtypeStruct((NBIN, LAGS), f32),
         ),
-        in_specs=[pl.BlockSpec(memory_space=pl.ANY), smem, smem, vmem],
+        in_specs=[pl.BlockSpec(memory_space=pl.ANY)] * 4,
         out_specs=(vmem, vmem, vmem),
         scratch_shapes=[
             *[pltpu.VMEM(block, bf16)] * Q,
+            pltpu.SMEM((1, 2), jnp.int32),
+            pltpu.SMEM((2,), jnp.int32),
+            pltpu.VMEM((1, 32 * CH), jnp.int32),
             pltpu.SMEM((1, 2), jnp.int32),
             pltpu.VMEM((Q * 2 * L, 12 * CH, 128), f32),
             pltpu.VMEM((2, CH, 128), f32),
@@ -444,6 +442,7 @@
             pltpu.VMEM((3, 3, 32, 256), bf16),
             pltpu.VMEM((2, 2, CH, LAGS), bf16),
             pltpu.SemaphoreType.DMA((Q,)),
+            pltpu.SemaphoreType.DMA((3,)),
             pltpu.SemaphoreType.DMA((copies,)),
             pltpu.SemaphoreType.DMA((copies,)),
         ],
@@ -455,9 +454,9 @@
 
 def local(spectra, band_offsets, window_keep, chan_dist):
     win_dev, ch_dev, _, freqs = spectra.shape
-    wt = spectra.reshape(win_dev, ch_dev, 2, freqs // 128, 128).transpose(0, 3, 2, 1, 4)
+    wt = spectra.transpose(0, 2, 1, 3)
     linear, phased, binned = stacks(wt, band_offsets, window_keep, chan_dist[None, :])
-    return (linear.transpose(1, 0, 2), phased.transpose(1, 0, 2), binned)
+    return linear, phased, binned
 
 
 def solution(mesh):

time: 71.4 us -> 69.4 us (0.972)
  local copies, waits for them, and re-layouts: 6.84 us -> 5.46 us
    reshape x2 -> x0, local copies, waits for them, and re-layouts: 3.12 us -> none  [local(): spectra.reshape(win_dev, ch_dev, 2, freqs // 128, 128)]
    unnamed x9 -> x10, local copies, waits for them, and re-layouts: 3.72 us -> 5.46 us
where the time goes in v5:
time: 69.4 us; the launch traced here: 69.3 us
  Pallas kernels  63.1 us (91%)
  local copies, waits for them, and re-layouts  5.46 us (8%)
    pallas_call x1, Pallas kernels, stacks(): pl.pallas_call(kernel, out_shape=(jax.ShapeDtypeStruct((CH, 2, LAGS), f32...  63.1 us
    unnamed x10, local copies, waits for them, and re-layouts  5.46 us

profile of v5, /device:TPU:2, one launch (start us, length us, event | category | flops | bytes accessed | tf_op | source)
XLA Modules:
  0.0 69.3 jit_solution(5438699341990090623)
XLA Ops:
  0.6 0.0 copy-start
  0.6 2.6 %copy.9 = bf16[2,64,2,2048]{3,1,2,0:T(8,128)(2,1)} copy(bf16[2,64,2,2048]{3,2,1,0:T(2,128)(2,1)} %param.4) | data formatting | bytes 2097152 | tf_op args[0]
  3.2 0.0 copy-start.1
  3.2 0.0 copy-start.2
  3.2 0.0 copy-done
  3.2 0.6 copy-done.1
  3.8 0.0 copy-done.2
  3.9 63.1 %shard_map.67 = (f32[64,2,1024]{2,1,0:T(2,128)S(1)}, f32[64,2,1024]{2,1,0:T(2,128)S(1)}, f32[32,1024]{1,0:T(8,128)S(1)}) custom-call(bf16[2,2,64,2048]{3,2,1,0:T(8,128)(2,1)} %bitcast.5, s32[1,2]{1,0:T(1,128)S(1)} %copy-done.1, s32[2]{0:T(128)S(1)} %copy-done.2, s32[1,2048]{1,0:T(1,128)S(1)} %bitcast.4), custom_call_target="tpu_custom_call" | custom-call | tf_op jit(solution)/shard_map/pallas_call | solution.py:409
  67.0 0.8 %copy.13 = f32[64,2,1024]{2,1,0:T(2,128)} copy(f32[64,2,1024]{2,1,0:T(2,128)S(1)} %get-tuple-element.6) | data formatting | bytes 1048576
  67.8 0.8 %copy.14 = f32[64,2,1024]{2,1,0:T(2,128)} copy(f32[64,2,1024]{2,1,0:T(2,128)S(1)} %get-tuple-element.7) | data formatting | bytes 1048576
  68.6 0.7 copy.15
Async XLA Ops:
  0.6 2.6 %copy-start = (s32[2048]{0:T(1024)S(1)}, s32[2048]{0:T(1024)}, u32[]{:S(2)}) copy-start(s32[2048]{0:T(1024)} %param.7) | copy-start | bytes 24580
  3.2 0.7 copy-start.1
  3.2 0.7 copy-start.2

commit v6 on v5

--- a/solution.py
+++ b/solution.py
@@ -9,6 +9,7 @@
 from jax.sharding import PartitionSpec as P
 
 LAGS = 1024
+HALF_LAGS = LAGS // 2
 NBIN = 32
 EPS = 1e-06
 FLOOR = 0.1
@@ -24,13 +25,13 @@
 
 
 def turn(product):
-    return jnp.bitwise_and(product, 2 * F - 1).astype(jnp.float32) * (math.pi / F)
+    return jnp.bitwise_and(product, 4 * F - 1).astype(jnp.float32) * (math.pi / (2 * F))
 
 
 def kernel(
     wt, offs_in, keep_in, dist_in,
     lin_out, ph_out, bin_out,
-    j0, j1, j2, j3, offs, keep, dist, far_offs, j32, power_m, power_o, member, ea, eb, table, x, acc,
+    j0, j1, j2, j3, offs, keep, dist, far_offs, j32, power_m, power_o, member, shift, flip, ea, eb, table, x, acc,
     s_early, s_late, ra_early, ra_late, pa_early, pa_late, rb, pb, ra2, rb2, g,
     local_sem, small_sem, send_sem, recv_sem,
 ):
@@ -125,25 +126,32 @@
         for_early[0].start()
         for_early[1].start()
 
-    lag = lax.broadcasted_iota(jnp.int32, (FINE, LAGS), 1) - LAGS // 2
-    row = lax.broadcasted_iota(jnp.int32, (FINE, LAGS), 0)
-    fine = turn(row * lag)
+    odd = 2 * lax.broadcasted_iota(jnp.int32, (FINE, HALF_LAGS), 1) + 1
+    row = lax.broadcasted_iota(jnp.int32, (FINE, HALF_LAGS), 0)
+    fine = turn(row * odd)
     eb[0] = jnp.cos(fine) * (1.0 / math.sqrt(F))
     eb[1] = jnp.sin(fine) * (1.0 / math.sqrt(F))
     for half in range(F // FINE // FINE):
-        coarse = turn((row + half * FINE) * FINE * lag)
+        coarse = turn((row + half * FINE) * FINE * odd)
         ea[0, half * FINE:(half + 1) * FINE] = jnp.cos(coarse)
         ea[1, half * FINE:(half + 1) * FINE] = jnp.sin(coarse)
+
+    step = lax.broadcasted_iota(jnp.int32, (8, F), 1).astype(jnp.float32) * (math.pi / (2 * F))
+    shift[0] = jnp.cos(step) * LIFT
+    shift[1] = jnp.sin(step) * LIFT
+    down_rows = lax.broadcasted_iota(jnp.int32, (HALF_LAGS, HALF_LAGS), 0)
+    along = lax.broadcasted_iota(jnp.int32, (HALF_LAGS, HALF_LAGS), 1)
+    flip[...] = (down_rows + along == HALF_LAGS - 1).astype(jnp.float32).astype(jnp.bfloat16)
 
     per = KQ // FINE
 
     def fill(a, _):
         ca = ea[0, pl.ds(a, 1), :]
         sa = ea[1, pl.ds(a, 1), :]
-        q2 = (a // per) * 2
+        chunk = a // per
         at = pl.ds(pl.multiple_of(lax.rem(a, per) * FINE, FINE), FINE)
-        table[q2, at, :] = (eb[0] * ca - eb[1] * sa).astype(jnp.bfloat16)
-        table[q2 + 1, at, :] = (eb[1] * ca + eb[0] * sa).astype(jnp.bfloat16)
+        table[chunk, at, :HALF_LAGS] = (eb[0] * ca - eb[1] * sa).astype(jnp.bfloat16)
+        table[chunk, at, HALF_LAGS:] = (eb[1] * ca + eb[0] * sa).astype(jnp.bfloat16)
         return 0
 
     far_first, mate_far = [], []
@@ -195,37 +203,32 @@
 
     def correlate(q, h, block, owns):
         at_m = pl.ds(pl.multiple_of((4 + block) * CH, CH), CH)
+        at_o = [
+            pl.ds((4 + block) * CH + jnp.where(owns, offs[0, k], far_offs[0, k]), CH) for k in range(2)
+        ]
+        sum_m, sum_o = None, [None, None]
+        for lg in range(L):
+            j = (q * L + lg) * 2
+            mr, mi = j32[j, at_m, :], j32[j + 1, at_m, :]
+            square = mr * mr + mi * mi
+            sum_m = square if sum_m is None else sum_m + square
+            first = (q * L + lg) * 128
+            cosine, sine = shift[0, 0:1, first:first + 128], shift[1, 0:1, first:first + 128]
+            mr, mi = mr * cosine + mi * sine, mi * cosine - mr * sine
+            one = slice(lg * 128, (lg + 1) * 128)
+            for k in range(2):
+                orr, oi = j32[j, at_o[k], :], j32[j + 1, at_o[k], :]
+                square = orr * orr + oi * oi
+                sum_o[k] = square if sum_o[k] is None else sum_o[k] + square
+                x[k * CH:(k + 1) * CH, one] = (mr * orr + mi * oi).astype(jnp.bfloat16)
+                x[(2 + k) * CH:(3 + k) * CH, one] = (mi * orr - mr * oi).astype(jnp.bfloat16)
+        power_m[h] = sum_m if q == 0 else power_m[h] + sum_m
         for k in range(2):
-            at_o = pl.ds((4 + block) * CH + jnp.where(owns, offs[0, k], far_offs[0, k]), CH)
-            sum_m, sum_o = None, None
-            for lg in range(L):
-                j = (q * L + lg) * 2
-                mr, mi = j32[j, at_m, :], j32[j + 1, at_m, :]
-                orr, oi = j32[j, at_o, :], j32[j + 1, at_o, :]
-                square = orr * orr + oi * oi
-                sum_o = square if sum_o is None else sum_o + square
-                if k == 0:
-                    square = mr * mr + mi * mi
-                    sum_m = square if sum_m is None else sum_m + square
-                mr, mi = mr * LIFT, mi * LIFT
-                real = (mr * orr + mi * oi).astype(jnp.bfloat16)
-                imag = (mi * orr - mr * oi).astype(jnp.bfloat16)
-                top = slice(k * CH, (k + 1) * CH)
-                low = slice((2 + k) * CH, (3 + k) * CH)
-                one = slice(lg * 128, (lg + 1) * 128)
-                two = slice(KQ + lg * 128, KQ + (lg + 1) * 128)
-                x[top, one] = real
-                x[top, two] = -imag
-                x[low, one] = imag
-                x[low, two] = real
-            power_o[h * 2 + k] = sum_o if q == 0 else power_o[h * 2 + k] + sum_o
-            if k == 0:
-                power_m[h] = sum_m if q == 0 else power_m[h] + sum_m
+            power_o[h * 2 + k] = sum_o[k] if q == 0 else power_o[h * 2 + k] + sum_o[k]
 
         def multiply(n, _):
             at = pl.ds(pl.multiple_of(n * 256, 256), 256)
-            value = jnp.dot(x[:, :KQ], table[2 * q, :, at], preferred_element_type=jnp.float32)
-            value += jnp.dot(x[:, KQ:], table[2 * q + 1, :, at], preferred_element_type=jnp.float32)
+            value = jnp.dot(x[...], table[q, :, at], preferred_element_type=jnp.float32)
             if q == 0:
                 acc[:, at] = value
             else:
@@ -244,8 +247,12 @@
                 mean_m = jnp.sum(power_m[h, at, :], axis=1, keepdims=True) * (1.0 / F)
                 mean_o = jnp.sum(power_o[h * 2 + k, at, :], axis=1, keepdims=True) * (1.0 / F)
                 gain = lax.rsqrt(mean_m + EPS) * (1.0 / LIFT) * lax.rsqrt(mean_o + EPS)
-                real = acc[pl.ds(pl.multiple_of(r, 16), 16), :] * gain
-                imag = acc[pl.ds(pl.multiple_of(2 * CH + r, 16), 16), :] * gain
+                even = acc[pl.ds(pl.multiple_of(r, 16), 16), :] * gain
+                swap = acc[pl.ds(pl.multiple_of(2 * CH + r, 16), 16), :] * gain
+                a, b = even[:, :HALF_LAGS], even[:, HALF_LAGS:]
+                c, d = swap[:, :HALF_LAGS], swap[:, HALF_LAGS:]
+                real = jnp.concatenate([a + d, a - d], axis=1)
+                imag = jnp.concatenate([c - b, c + b], axis=1)
                 scale = weight * jnp.minimum(lax.rsqrt(real * real + imag * imag), 1.0 / FLOOR)
                 s[0, k, at, :] = (weight * real).astype(jnp.bfloat16)
                 s[1, k, at, :] = (scale * real).astype(jnp.bfloat16)
@@ -362,11 +369,12 @@
         mate_far[q].wait_recv()
         for copy in forward[q]:
             copy.wait_recv()
+        widen(q, 2, 8)
         for_early[q].wait_recv()
         pos = 10 - 9 * core
         pass_on.append(send(joined[q].at[pos], joined[q].at[pos], near(mate)))
         for_late[q].start()
-        widen(q, 2 - core, 9)
+        widen(q, 10 - 9 * core, 1)
         correlate(q, 0, early, owns_early)
     stack(0, s_early)
     early_first = first_sums(s_early, ra_early, owns_early)
@@ -384,16 +392,22 @@
 
     for copy in last_a + last_b:
         copy.wait_recv()
+    bins_low = jnp.zeros((128, HALF_LAGS), jnp.float32)
+    bins_high = jnp.zeros((128, HALF_LAGS), jnp.float32)
     for k in range(2):
-        lin_out[:, k, :] = g[0, k].astype(jnp.float32)
-        ph_out[:, k, :] = g[1, k].astype(jnp.float32)
-    bins = jnp.zeros((128, LAGS), jnp.float32)
-    for k in range(2):
-        bins += lax.dot_general(
-            member[k].astype(jnp.bfloat16), g[0, k], (((0,), (0,)), ((), ())),
-            preferred_element_type=jnp.float32,
-        )
-    bin_out[...] = bins[:NBIN]
+        for out, v in ((lin_out, 0), (ph_out, 1)):
+            low = jnp.dot(g[v, k, :, :HALF_LAGS], flip[...], preferred_element_type=jnp.float32)
+            high = g[v, k, :, HALF_LAGS:]
+            out[:, k, :HALF_LAGS] = low
+            out[:, k, HALF_LAGS:] = high.astype(jnp.float32)
+            if v == 0:
+                column = member[k].astype(jnp.bfloat16)
+                sides = (((0,), (0,)), ((), ()))
+                bins_low += lax.dot_general(
+                    column, low.astype(jnp.bfloat16), sides, preferred_element_type=jnp.float32)
+                bins_high += lax.dot_general(column, high, sides, preferred_element_type=jnp.float32)
+    bin_out[:, :HALF_LAGS] = bins_low[:NBIN]
+    bin_out[:, HALF_LAGS:] = bins_high[:NBIN]
     for when, copy in sent:
         if when is None:
             copy.wait_send()
@@ -413,7 +427,7 @@
             jax.ShapeDtypeStruct((CH, 2, LAGS), f32),
             jax.ShapeDtypeStruct((NBIN, LAGS), f32),
         ),
-        in_specs=[pl.BlockSpec(memory_space=pl.ANY)] * 4,
+        in_specs=[pl.BlockSpec(memory_space=pl.ANY)] + [pl.BlockSpec(memory_space=pltpu.HBM)] * 3,
         out_specs=(vmem, vmem, vmem),
         scratch_shapes=[
             *[pltpu.VMEM(block, bf16)] * Q,
@@ -425,10 +439,12 @@
             pltpu.VMEM((2, CH, 128), f32),
             pltpu.VMEM((4, CH, 128), f32),
             pltpu.VMEM((2, CH, 128), f32),
-            pltpu.VMEM((2, F // FINE, LAGS), f32),
-            pltpu.VMEM((2, FINE, LAGS), f32),
-            pltpu.VMEM((2 * Q, KQ, LAGS), bf16),
-            pltpu.VMEM((4 * CH, 2 * KQ), bf16),
+            pltpu.VMEM((2, 8, F), f32),
+            pltpu.VMEM((HALF_LAGS, HALF_LAGS), bf16),
+            pltpu.VMEM((2, F // FINE, HALF_LAGS), f32),
+            pltpu.VMEM((2, FINE, HALF_LAGS), f32),
+            pltpu.VMEM((Q, KQ, LAGS), bf16),
+            pltpu.VMEM((4 * CH, KQ), bf16),
             pltpu.VMEM((4 * CH, LAGS), f32),
             pltpu.VMEM((3, 2, CH, LAGS), bf16),
             pltpu.VMEM((3, 2, CH, LAGS), bf16),

time: 69.4 us -> 66.8 us (0.963)
  Pallas kernels: 63.1 us -> 60.1 us
    pallas_call x1, Pallas kernels: 63.1 us -> 60.1 us  [stacks(): pl.pallas_call(kernel, out_shape=(jax.ShapeDtypeStruct((CH, 2, LAGS), f32...]
where the time goes in v6:
time: 66.8 us; the launch traced here: 66.2 us
  Pallas kernels  60.1 us (90%)
  local copies, waits for them, and re-layouts  5.46 us (8%)
    pallas_call x1, Pallas kernels, stacks(): pl.pallas_call(kernel, out_shape=(jax.ShapeDtypeStruct((CH, 2, LAGS), f32...  60.1 us
    unnamed x10, local copies, waits for them, and re-layouts  5.46 us

profile of v6, /device:TPU:2, one launch (start us, length us, event | category | flops | bytes accessed | tf_op | source)
XLA Modules:
  0.0 66.2 jit_solution(7203066495950171093)
XLA Ops:
  0.6 0.0 copy-start
  0.6 2.6 %copy.9 = bf16[2,64,2,2048]{3,1,2,0:T(8,128)(2,1)} copy(bf16[2,64,2,2048]{3,2,1,0:T(2,128)(2,1)} %param.4) | data formatting | bytes 2097152 | tf_op args[0]
  3.2 0.0 copy-start.1
  3.2 0.0 copy-start.2
  3.2 0.0 copy-done
  3.2 0.6 copy-done.1
  3.8 0.0 copy-done.2
  3.9 60.1 %shard_map.67 = (f32[64,2,1024]{2,1,0:T(2,128)S(1)}, f32[64,2,1024]{2,1,0:T(2,128)S(1)}, f32[32,1024]{1,0:T(8,128)S(1)}) custom-call(bf16[2,2,64,2048]{3,2,1,0:T(8,128)(2,1)} %bitcast.5, s32[1,2]{1,0:T(1,128)S(1)} %copy-done.1, s32[2]{0:T(128)S(1)} %copy-done.2, s32[1,2048]{1,0:T(1,128)S(1)} %bitcast.4), custom_call_target="tpu_custom_call" | custom-call | tf_op jit(solution)/shard_map/pallas_call | solution.py:423
  63.9 0.8 %copy.13 = f32[64,2,1024]{2,1,0:T(2,128)} copy(f32[64,2,1024]{2,1,0:T(2,128)S(1)} %get-tuple-element.6) | data formatting | bytes 1048576
  64.7 0.8 %copy.14 = f32[64,2,1024]{2,1,0:T(2,128)} copy(f32[64,2,1024]{2,1,0:T(2,128)S(1)} %get-tuple-element.7) | data formatting | bytes 1048576
  65.5 0.7 copy.15
Async XLA Ops:
  0.6 2.6 %copy-start = (s32[2048]{0:T(1024)S(1)}, s32[2048]{0:T(1024)}, u32[]{:S(2)}) copy-start(s32[2048]{0:T(1024)} %param.7) | copy-start | bytes 24580
  3.2 0.7 copy-start.1
  3.2 0.7 %copy-start.2 = (s32[2]{0:T(128)S(1)}, s32[2]{0:T(128)}, u32[]{:S(2)}) copy-start(s32[2]{0:T(128)} %keep_in.1) | copy-start | bytes 28

commit v7 on v6

--- a/solution.py
+++ b/solution.py
@@ -66,7 +66,7 @@
     ]
     y_half = [1 - yhi, yhi, 1 - yhi]
     far_x = [{"chan": chan, "win": p * 2 + 1 - yhi} for p in x_peer]
-    g_dev = [y_dev[0]] + x_dev + far_x
+    g_dev = [far_x[1], far_x[0], far_x[2], x_dev[1], y_dev[0], x_dev[0], x_dev[2]]
 
     small = [
         pltpu.make_async_copy(source, target, small_sem.at[n])
@@ -267,9 +267,6 @@
     def rows32(i):
         return pl.ds(pl.multiple_of(i * 32, 32), 32)
 
-    def cols512(i):
-        return pl.ds(pl.multiple_of(i * 512, 512), 512)
-
     def cols256(i):
         return pl.ds(pl.multiple_of(i * 256, 256), 256)
 
@@ -304,7 +301,7 @@
             for d in range(3):
                 total += ra[d, v].astype(jnp.float32)
             pa[v] = total.astype(jnp.bfloat16)
-        a2 = to_owners(lambda half: pa.at[:, :, cols512(half)], ra2, owns)
+        a2 = to_owners(lambda half: pa, ra2, owns)
         b2 = [make(pb.at[:, :, cols256(x_peer[d])], rb2.at[d], x_dev[d], when=owns) for d in range(3)]
 
         @pl.when(owns)
@@ -326,9 +323,9 @@
         phased = linear * jnp.sqrt(parts[1] * parts[1] + parts[2] * parts[2]) * (1.0 / 16.0)
         return linear.astype(jnp.bfloat16), phased.astype(jnp.bfloat16)
 
-    piece_a = g.at[:, 0, rows16(xx), cols512(yhi)]
+    piece_a = g.at[:, 0, rows16(xx), :]
     piece_b = g.at[:, 1, rows32(yhi), cols256(xx)]
-    last_a = [make(piece_a, piece_a, dev) for dev in g_dev]
+    last_a = [make(piece_a, piece_a, dev) for dev in x_dev]
     last_b = [make(piece_b, piece_b, dev) for dev in g_dev]
 
     def results(pa, owns, copies):
@@ -340,13 +337,13 @@
                 copy.wait_recv()
             parts = []
             for v in range(3):
-                total = pa[v, :, cols512(yhi)].astype(jnp.float32)
+                total = pa[v].astype(jnp.float32)
                 for d in range(3):
                     total += ra2[d, v].astype(jnp.float32)
                 parts.append(total)
             linear, phased = finish(parts)
-            g[0, 0, rows16(xx), cols512(yhi)] = linear
-            g[1, 0, rows16(xx), cols512(yhi)] = phased
+            g[0, 0, rows16(xx), :] = linear
+            g[1, 0, rows16(xx), :] = phased
             for copy in last_a:
                 copy.start()
             for copy in b2:
@@ -390,11 +387,11 @@
     results(pa_early, owns_early, early_second)
     results(pa_late, owns_late, late_second)
 
-    for copy in last_a + last_b:
-        copy.wait_recv()
     bins_low = jnp.zeros((128, HALF_LAGS), jnp.float32)
     bins_high = jnp.zeros((128, HALF_LAGS), jnp.float32)
     for k in range(2):
+        for copy in (last_a, last_b)[k]:
+            copy.wait_recv()
         for out, v in ((lin_out, 0), (ph_out, 1)):
             low = jnp.dot(g[v, k, :, :HALF_LAGS], flip[...], preferred_element_type=jnp.float32)
             high = g[v, k, :, HALF_LAGS:]
@@ -418,7 +415,7 @@
 def stacks(wt, offs, keep, dist):
     vmem = pl.BlockSpec(memory_space=pltpu.VMEM)
     bf16, f32 = jnp.bfloat16, jnp.float32
-    copies = 1 + 10 * Q + 2 * 12 + 14
+    copies = 1 + 10 * Q + 2 * 12 + 10
     block = (12, 2, CH, KQ)
     return pl.pallas_call(
         kernel,
@@ -454,7 +451,7 @@
             pltpu.VMEM((3, 16, LAGS), bf16),
             pltpu.VMEM((3, 3, 32, LAGS), bf16),
             pltpu.VMEM((3, 32, LAGS), bf16),
-            pltpu.VMEM((3, 3, 16, 512), bf16),
+            pltpu.VMEM((3, 3, 16, LAGS), bf16),
             pltpu.VMEM((3, 3, 32, 256), bf16),
             pltpu.VMEM((2, 2, CH, LAGS), bf16),
             pltpu.SemaphoreType.DMA((Q,)),

time: 66.8 us -> 65.9 us (0.987)
  no operation moved by 1% of the time
where the time goes in v7:
time: 65.9 us; the launch traced here: 65.8 us
  Pallas kernels  59.6 us (90%)
  local copies, waits for them, and re-layouts  5.46 us (8%)
    pallas_call x1, Pallas kernels, stacks(): pl.pallas_call(kernel, out_shape=(jax.ShapeDtypeStruct((CH, 2, LAGS), f32...  59.6 us
    unnamed x10, local copies, waits for them, and re-layouts  5.46 us

profile of v7, /device:TPU:2, one launch (start us, length us, event | category | flops | bytes accessed | tf_op | source)
XLA Modules:
  0.0 65.8 jit_solution(12476762285271046917)
XLA Ops:
  0.6 0.0 copy-start
  0.6 2.6 %copy.9 = bf16[2,64,2,2048]{3,1,2,0:T(8,128)(2,1)} copy(bf16[2,64,2,2048]{3,2,1,0:T(2,128)(2,1)} %param.4) | data formatting | bytes 2097152 | tf_op args[0]
  3.2 0.0 copy-start.1
  3.2 0.0 copy-start.2
  3.2 0.0 copy-done
  3.2 0.6 copy-done.1
  3.8 0.0 copy-done.2
  3.9 59.6 %shard_map.67 = (f32[64,2,1024]{2,1,0:T(2,128)S(1)}, f32[64,2,1024]{2,1,0:T(2,128)S(1)}, f32[32,1024]{1,0:T(8,128)S(1)}) custom-call(bf16[2,2,64,2048]{3,2,1,0:T(8,128)(2,1)} %bitcast.5, s32[1,2]{1,0:T(1,128)S(1)} %copy-done.1, s32[2]{0:T(128)S(1)} %copy-done.2, s32[1,2048]{1,0:T(1,128)S(1)} %bitcast.4), custom_call_target="tpu_custom_call" | custom-call | tf_op jit(solution)/shard_map/pallas_call | solution.py:420
  63.5 0.8 %copy.13 = f32[64,2,1024]{2,1,0:T(2,128)} copy(f32[64,2,1024]{2,1,0:T(2,128)S(1)} %get-tuple-element.6) | data formatting | bytes 1048576
  64.3 0.8 %copy.14 = f32[64,2,1024]{2,1,0:T(2,128)} copy(f32[64,2,1024]{2,1,0:T(2,128)S(1)} %get-tuple-element.7) | data formatting | bytes 1048576
  65.1 0.7 copy.15
Async XLA Ops:
  0.6 2.6 %copy-start = (s32[2048]{0:T(1024)S(1)}, s32[2048]{0:T(1024)}, u32[]{:S(2)}) copy-start(s32[2048]{0:T(1024)} %param.7) | copy-start | bytes 24580
  3.2 0.7 copy-start.1
  3.2 0.7 %copy-start.2 = (s32[2]{0:T(128)S(1)}, s32[2]{0:T(128)}, u32[]{:S(2)}) copy-start(s32[2]{0:T(128)} %keep_in.1) | copy-start | bytes 28

commit v8 on v7

--- a/solution.py
+++ b/solution.py
@@ -227,7 +227,7 @@
             power_o[h * 2 + k] = sum_o[k] if q == 0 else power_o[h * 2 + k] + sum_o[k]
 
         def multiply(n, _):
-            at = pl.ds(pl.multiple_of(n * 256, 256), 256)
+            at = pl.ds(pl.multiple_of(n * 512, 512), 512)
             value = jnp.dot(x[...], table[q, :, at], preferred_element_type=jnp.float32)
             if q == 0:
                 acc[:, at] = value
@@ -235,31 +235,30 @@
                 acc[:, at] += value
             return 0
 
-        lax.fori_loop(0, LAGS // 256, multiply, 0)
+        lax.fori_loop(0, LAGS // 512, multiply, 0)
 
     weight = jnp.where(ylo == 0, keep[0], keep[1]).astype(jnp.float32)
 
-    def stack(h, s):
-        for k in range(2):
-            def one(i, _):
-                r = k * CH + i * 16
-                at = pl.ds(pl.multiple_of(i * 16, 16), 16)
-                mean_m = jnp.sum(power_m[h, at, :], axis=1, keepdims=True) * (1.0 / F)
-                mean_o = jnp.sum(power_o[h * 2 + k, at, :], axis=1, keepdims=True) * (1.0 / F)
-                gain = lax.rsqrt(mean_m + EPS) * (1.0 / LIFT) * lax.rsqrt(mean_o + EPS)
-                even = acc[pl.ds(pl.multiple_of(r, 16), 16), :] * gain
-                swap = acc[pl.ds(pl.multiple_of(2 * CH + r, 16), 16), :] * gain
-                a, b = even[:, :HALF_LAGS], even[:, HALF_LAGS:]
-                c, d = swap[:, :HALF_LAGS], swap[:, HALF_LAGS:]
-                real = jnp.concatenate([a + d, a - d], axis=1)
-                imag = jnp.concatenate([c - b, c + b], axis=1)
-                scale = weight * jnp.minimum(lax.rsqrt(real * real + imag * imag), 1.0 / FLOOR)
-                s[0, k, at, :] = (weight * real).astype(jnp.bfloat16)
-                s[1, k, at, :] = (scale * real).astype(jnp.bfloat16)
-                s[2, k, at, :] = (scale * imag).astype(jnp.bfloat16)
-                return 0
-
-            lax.fori_loop(0, CH // 16, one, 0)
+    def stack(h, s, k):
+        def one(i, _):
+            r = k * CH + i * 16
+            at = pl.ds(pl.multiple_of(i * 16, 16), 16)
+            mean_m = jnp.sum(power_m[h, at, :], axis=1, keepdims=True) * (1.0 / F)
+            mean_o = jnp.sum(power_o[h * 2 + k, at, :], axis=1, keepdims=True) * (1.0 / F)
+            gain = lax.rsqrt(mean_m + EPS) * (1.0 / LIFT) * lax.rsqrt(mean_o + EPS)
+            even = acc[pl.ds(pl.multiple_of(r, 16), 16), :] * gain
+            swap = acc[pl.ds(pl.multiple_of(2 * CH + r, 16), 16), :] * gain
+            a, b = even[:, :HALF_LAGS], even[:, HALF_LAGS:]
+            c, d = swap[:, :HALF_LAGS], swap[:, HALF_LAGS:]
+            real = jnp.concatenate([a + d, a - d], axis=1)
+            imag = jnp.concatenate([c - b, c + b], axis=1)
+            scale = weight * jnp.minimum(lax.rsqrt(real * real + imag * imag), 1.0 / FLOOR)
+            s[0, k, at, :] = (weight * real).astype(jnp.bfloat16)
+            s[1, k, at, :] = (scale * real).astype(jnp.bfloat16)
+            s[2, k, at, :] = (scale * imag).astype(jnp.bfloat16)
+            return 0
+
+        lax.fori_loop(0, CH // 16, one, 0)
 
     def rows16(i):
         return pl.ds(pl.multiple_of(i * 16, 16), 16)
@@ -287,10 +286,12 @@
 
         return copies
 
-    def first_sums(s, ra, owns):
-        a = [send(s.at[:, 0, rows16(x_peer[d]), :], ra.at[d], x_dev[d]) for d in range(3)]
+    def first_sums(h, s, ra, owns):
+        stack(h, s, 1)
         b = to_owners(lambda half: s.at[:, 1, rows32(half), :], rb, owns)
-        return a, b
+        stack(h, s, 0)
+        a = {d: send(s.at[:, 0, rows16(x_peer[d]), :], ra.at[d], x_dev[d]) for d in (1, 0, 2)}
+        return list(a.values()), b
 
     def second_sums(s, ra, pa, owns, copies):
         a, b = copies
@@ -373,15 +374,13 @@
         for_late[q].start()
         widen(q, 10 - 9 * core, 1)
         correlate(q, 0, early, owns_early)
-    stack(0, s_early)
-    early_first = first_sums(s_early, ra_early, owns_early)
+    early_first = first_sums(0, s_early, ra_early, owns_early)
     for q in range(Q):
         pass_on[q].wait_recv()
         for_late[q].wait_recv()
         widen(q, 10 * core, 2)
         correlate(q, 1, late, owns_late)
-    stack(1, s_late)
-    late_first = first_sums(s_late, ra_late, owns_late)
+    late_first = first_sums(1, s_late, ra_late, owns_late)
     early_second = second_sums(s_early, ra_early, pa_early, owns_early, early_first)
     late_second = second_sums(s_late, ra_late, pa_late, owns_late, late_first)
     results(pa_early, owns_early, early_second)

time: 65.9 us -> 64.5 us (0.979)
  Pallas kernels: 59.6 us -> 58.1 us
    pallas_call x1, Pallas kernels: 59.6 us -> 58.1 us  [stacks(): pl.pallas_call(kernel, out_shape=(jax.ShapeDtypeStruct((CH, 2, LAGS), f32...]
where the time goes in v8:
time: 64.5 us; the launch traced here: 64.2 us
  Pallas kernels  58.1 us (90%)
  local copies, waits for them, and re-layouts  5.46 us (8%)
  between operations  0.65 us (1%)
    pallas_call x1, Pallas kernels, stacks(): pl.pallas_call(kernel, out_shape=(jax.ShapeDtypeStruct((CH, 2, LAGS), f32...  58.1 us
    unnamed x10, local copies, waits for them, and re-layouts  5.46 us

profile of v8, /device:TPU:2, one launch (start us, length us, event | category | flops | bytes accessed | tf_op | source)
XLA Modules:
  0.0 64.2 jit_solution(17442722784519396983)
XLA Ops:
  0.6 0.0 copy-start
  0.6 2.6 %copy.9 = bf16[2,64,2,2048]{3,1,2,0:T(8,128)(2,1)} copy(bf16[2,64,2,2048]{3,2,1,0:T(2,128)(2,1)} %param.4) | data formatting | bytes 2097152 | tf_op args[0]
  3.2 0.0 copy-start.1
  3.2 0.0 copy-start.2
  3.2 0.0 copy-done
  3.2 0.6 %copy-done.1 = s32[1,2]{1,0:T(1,128)S(1)} copy-done((s32[1,2]{1,0:T(1,128)S(1)}, s32[1,2]{1,0:T(1,128)}, u32[]{:S(2)}) %copy-start.1) | copy-done | bytes 32
  3.8 0.0 copy-done.2
  3.9 58.1 %shard_map.67 = (f32[64,2,1024]{2,1,0:T(2,128)S(1)}, f32[64,2,1024]{2,1,0:T(2,128)S(1)}, f32[32,1024]{1,0:T(8,128)S(1)}) custom-call(bf16[2,2,64,2048]{3,2,1,0:T(8,128)(2,1)} %bitcast.5, s32[1,2]{1,0:T(1,128)S(1)} %copy-done.1, s32[2]{0:T(128)S(1)} %copy-done.2, s32[1,2048]{1,0:T(1,128)S(1)} %bitcast.4), custom_call_target="tpu_custom_call" | custom-call | tf_op jit(solution)/shard_map/pallas_call | solution.py:419
  62.0 0.8 %copy.13 = f32[64,2,1024]{2,1,0:T(2,128)} copy(f32[64,2,1024]{2,1,0:T(2,128)S(1)} %get-tuple-element.6) | data formatting | bytes 1048576
  62.8 0.8 %copy.14 = f32[64,2,1024]{2,1,0:T(2,128)} copy(f32[64,2,1024]{2,1,0:T(2,128)S(1)} %get-tuple-element.7) | data formatting | bytes 1048576
  63.6 0.7 %copy.15 = f32[32,1024]{1,0:T(8,128)} copy(f32[32,1024]{1,0:T(8,128)S(1)} %get-tuple-element.8) | data formatting | bytes 262144
Async XLA Ops:
  0.6 2.6 %copy-start = (s32[2048]{0:T(1024)S(1)}, s32[2048]{0:T(1024)}, u32[]{:S(2)}) copy-start(s32[2048]{0:T(1024)} %param.7) | copy-start | bytes 24580
  3.2 0.7 %copy-start.1 = (s32[1,2]{1,0:T(1,128)S(1)}, s32[1,2]{1,0:T(1,128)}, u32[]{:S(2)}) copy-start(s32[1,2]{1,0:T(1,128)} %offs_in.1) | copy-start | bytes 28
  3.2 0.7 %copy-start.2 = (s32[2]{0:T(128)S(1)}, s32[2]{0:T(128)}, u32[]{:S(2)}) copy-start(s32[2]{0:T(128)} %keep_in.1) | copy-start | bytes 28

commit v9 on v8

--- a/solution.py
+++ b/solution.py
@@ -227,7 +227,7 @@
             power_o[h * 2 + k] = sum_o[k] if q == 0 else power_o[h * 2 + k] + sum_o[k]
 
         def multiply(n, _):
-            at = pl.ds(pl.multiple_of(n * 512, 512), 512)
+            at = pl.ds(pl.multiple_of(n * 1024, 1024), 1024)
             value = jnp.dot(x[...], table[q, :, at], preferred_element_type=jnp.float32)
             if q == 0:
                 acc[:, at] = value
@@ -235,7 +235,7 @@
                 acc[:, at] += value
             return 0
 
-        lax.fori_loop(0, LAGS // 512, multiply, 0)
+        lax.fori_loop(0, LAGS // 1024, multiply, 0)
 
     weight = jnp.where(ylo == 0, keep[0], keep[1]).astype(jnp.float32)
 

time: 64.5 us -> 64.5 us (level)
  no operation moved by 1% of the time
where the time goes in v9:
time: 64.5 us
  Pallas kernels  58.4 us (91%)
  local copies, waits for them, and re-layouts  5.46 us (8%)
  between operations  0.65 us (1%)
    pallas_call x1, Pallas kernels, stacks(): pl.pallas_call(kernel, out_shape=(jax.ShapeDtypeStruct((CH, 2, LAGS), f32...  58.4 us
    unnamed x10, local copies, waits for them, and re-layouts  5.46 us

profile of v9, /device:TPU:2, one launch (start us, length us, event | category | flops | bytes accessed | tf_op | source)
XLA Modules:
  0.0 64.5 jit_solution(16788165965829896801)
XLA Ops:
  0.6 0.0 copy-start
  0.6 2.6 %copy.9 = bf16[2,64,2,2048]{3,1,2,0:T(8,128)(2,1)} copy(bf16[2,64,2,2048]{3,2,1,0:T(2,128)(2,1)} %param.4) | data formatting | bytes 2097152 | tf_op args[0]
  3.2 0.0 copy-start.1
  3.2 0.0 copy-start.2
  3.2 0.0 copy-done
  3.2 0.6 %copy-done.1 = s32[1,2]{1,0:T(1,128)S(1)} copy-done((s32[1,2]{1,0:T(1,128)S(1)}, s32[1,2]{1,0:T(1,128)}, u32[]{:S(2)}) %copy-start.1) | copy-done | bytes 32
  3.8 0.0 copy-done.2
  3.9 58.4 %shard_map.67 = (f32[64,2,1024]{2,1,0:T(2,128)S(1)}, f32[64,2,1024]{2,1,0:T(2,128)S(1)}, f32[32,1024]{1,0:T(8,128)S(1)}) custom-call(bf16[2,2,64,2048]{3,2,1,0:T(8,128)(2,1)} %bitcast.5, s32[1,2]{1,0:T(1,128)S(1)} %copy-done.1, s32[2]{0:T(128)S(1)} %copy-done.2, s32[1,2048]{1,0:T(1,128)S(1)} %bitcast.4), custom_call_target="tpu_custom_call" | custom-call | tf_op jit(solution)/shard_map/pallas_call | solution.py:419
  62.2 0.8 %copy.13 = f32[64,2,1024]{2,1,0:T(2,128)} copy(f32[64,2,1024]{2,1,0:T(2,128)S(1)} %get-tuple-element.6) | data formatting | bytes 1048576
  63.0 0.8 %copy.14 = f32[64,2,1024]{2,1,0:T(2,128)} copy(f32[64,2,1024]{2,1,0:T(2,128)S(1)} %get-tuple-element.7) | data formatting | bytes 1048576
  63.8 0.7 %copy.15 = f32[32,1024]{1,0:T(8,128)} copy(f32[32,1024]{1,0:T(8,128)S(1)} %get-tuple-element.8) | data formatting | bytes 262144
Async XLA Ops:
  0.6 2.6 %copy-start = (s32[2048]{0:T(1024)S(1)}, s32[2048]{0:T(1024)}, u32[]{:S(2)}) copy-start(s32[2048]{0:T(1024)} %param.7) | copy-start | bytes 24580
  3.2 0.7 %copy-start.1 = (s32[1,2]{1,0:T(1,128)S(1)}, s32[1,2]{1,0:T(1,128)}, u32[]{:S(2)}) copy-start(s32[1,2]{1,0:T(1,128)} %offs_in.1) | copy-start | bytes 28
  3.2 0.7 %copy-start.2 = (s32[2]{0:T(128)S(1)}, s32[2]{0:T(128)}, u32[]{:S(2)}) copy-start(s32[2]{0:T(128)} %keep_in.1) | copy-start | bytes 28
